TPU v7x, 32 devices: a whole 2x2x4 slice. The times are simulated.
32 devices in a mesh: pipe: 4 (over y, core), ctx: 2 (over x), tp: 4 (over z).
Axes of the slice: x: 2, y: 2, z: 4, core: 2. Of those that a mesh axis runs over, the one named last changes fastest.
Arguments:
- hidden_in: bfloat16 [4, 256, 4096], P('pipe', 'ctx', 'tp'), may hold values from -8 to 8
- doc_ids: int32 [256], P('ctx'), may hold values from 0 to 3, never falling along the last dimension, each value on 1 to 128 neighbouring positions
- layer_kind: int32 [4], P('pipe'), may hold values from 0 to 1, as said below
- norm_gain: float32 [4, 4096], P('pipe', 'tp'), may hold values from 0.5 to 1.5
- q_weight: bfloat16 [4, 4096, 4096], P('pipe', 'ctx', 'tp'), may hold values from -2 to 2
- k_weight: bfloat16 [4, 4096, 512], P('pipe', 'ctx', 'tp'), may hold values from -1 to 1
- v_weight: bfloat16 [4, 4096, 512], P('pipe', 'ctx', 'tp'), may hold values from -0.09375 to 0.09375
- bc_weight: bfloat16 [4, 4096, 32], P('pipe', 'tp'), may hold values from -0.046875 to 0.046875
- dt_weight: bfloat16 [4, 4096, 64], P('pipe', 'tp'), may hold values from -0.09375 to 0.09375
- dt_bias: float32 [4, 64], P('pipe', 'tp'), may hold values from -1 to 1
- decay_rate: float32 [4, 64], P('pipe', 'tp'), may hold values from 0.0001953125 to 0.05
- skip_gain: float32 [4, 64], P('pipe', 'tp'), may hold values from 0.5 to 1.5
Outputs:
- section_out: bfloat16 [4, 256, 4096], P('pipe', 'ctx', 'tp')
- passed: bfloat16 [4, 256, 4096], P('pipe', 'ctx', 'tp')
Inputs may be any that keep to these rules, and one draw needn't show every extreme that they name: `layer_kind`: every draw has at least one attention section and at least one state-space section.
All inputs are finite; a program needn't handle non-finite values.
Results may differ from a plain program's by a relative error of at most 0.011.
Values may be sent and summed in bfloat16 or wider, within the bound.
A program may use at most 64 MiB of HBM per device.

v0:
```python
import jax
import jax.numpy as jnp
from jax import lax
from jax.sharding import PartitionSpec as P

D = 4096
HD = 128


def entering(x, axis, combine, identity):
    devices, index = (lax.axis_size(axis), lax.axis_index(axis))
    everything = jax.tree.map(
        lambda part, kind: lax.all_gather(part.astype(kind), axis), x, (jnp.bfloat16, jnp.bfloat16)
    )
    start = jax.tree.map(
        lambda part, zero: jnp.broadcast_to(jnp.asarray(zero, part.dtype), part.shape), x, identity
    )

    def turn(k, before):
        reached = k < index
        new = combine(
            before, jax.tree.map(lambda part, own: part[k].astype(own.dtype), everything, x)
        )
        return jax.tree.map(lambda a, b: jnp.where(reached, a, b), new, before)

    return lax.fori_loop(0, devices, turn, start)


def passed_along(x, axis, by):
    devices = lax.axis_size(axis)
    pairs = [(i, i + by) for i in range(devices) if 0 <= i + by < devices]
    return lax.ppermute(x, axis, pairs)


def make_fold(q_rows, q_pos, q_ids, ids_all, groups, head_size, active):
    rows = q_rows.shape[0]
    gsize = rows // groups
    q_top = jnp.max(q_pos.reshape(groups, gsize), axis=1)
    scale = head_size ** (-0.5)

    def update(state, piece_k, piece_v, key_pos, key_ids):
        top, denom, total = state
        scores = (
            jnp.einsum("tkjd,skd->kjts", q_rows, piece_k, preferred_element_type=jnp.float32)
            * scale
        )
        allowed = (key_pos[None, :] <= q_pos[:, None]) & (key_ids[None, :] == q_ids[:, None])
        scores = jnp.where(allowed[None, None], scores, -1e30)
        new_top = jnp.maximum(top, jnp.max(scores, axis=-1))
        probs = jnp.where(allowed[None, None], jnp.exp(scores - new_top[..., None]), 0.0)
        factor = jnp.exp(top - new_top)
        denom = denom * factor + jnp.sum(probs, axis=-1)
        total = total * factor[..., None] + jnp.einsum(
            "kjts,skd->kjtd",
            probs.astype(jnp.bfloat16),
            piece_v,
            preferred_element_type=jnp.float32,
        )
        return (new_top, denom, total)

    def fold(carry, piece, start):
        piece_k, piece_v = piece
        count = piece_k.shape[0]
        block = 512 if count % 512 == 0 else count
        for offset in range(0, count, block):
            key_start = start + offset
            key_pos = key_start + jnp.arange(block)
            key_ids = lax.dynamic_slice_in_dim(ids_all, key_start, block)
            block_k = piece_k[offset : offset + block]
            block_v = piece_v[offset : offset + block]
            low = 0

            def compute(state, low=low):
                return update(state, block_k, block_v, key_pos, key_ids)

            wanted = jnp.logical_and(active, key_start <= q_top[0])
            updated = [lax.cond(wanted, compute, lambda state: state, carry[0])]
            carry = tuple(updated)
        return carry

    def initial(kv_count, group):
        return tuple(
            (
                (
                    jnp.full((kv_count, group, gsize), -1e30, jnp.float32),
                    jnp.zeros((kv_count, group, gsize), jnp.float32),
                    jnp.zeros((kv_count, group, gsize, head_size), jnp.float32),
                )
                for index in range(groups)
            )
        )

    def finish(carry):
        parts = [
            total / jnp.where(denom > 0.0, denom, 1.0)[..., None] for top, denom, total in carry
        ]
        joined = parts[0]
        kv_count, group = (joined.shape[0], joined.shape[1])
        return (
            jnp.transpose(joined, (2, 0, 1, 3))
            .reshape(rows, kv_count * group * head_size)
            .astype(jnp.bfloat16)
        )

    return (fold, initial, finish)


def shards(
    hidden_in,
    doc_ids,
    layer_kind,
    norm_gain,
    q_weight,
    k_weight,
    v_weight,
    bc_weight,
    dt_weight,
    dt_bias,
    decay_rate,
    skip_gain,
):
    current = hidden_in[0]
    rows, width = current.shape
    ctx_pos = lax.axis_index("ctx")
    tp_pos = lax.axis_index("tp")
    ids_all = lax.all_gather(doc_ids, "ctx", axis=0, tiled=True)
    first = ctx_pos * rows
    prev_id = jnp.where(
        ctx_pos > 0,
        lax.dynamic_index_in_dim(ids_all, jnp.maximum(first - 1, 0), 0, keepdims=False),
        -1,
    )
    gain = norm_gain[0]
    head_size = HD
    q_cols = q_weight.shape[2]
    kv_cols = k_weight.shape[2]
    heads_local = q_cols // head_size
    kv_local = kv_cols // head_size
    group = heads_local // kv_local
    is_attention = layer_kind[0] == 1
    hf = current.astype(jnp.float32)
    squares = lax.psum(jnp.sum(hf * hf, axis=1), "tp")
    xn = (hf * lax.rsqrt(squares / D + 1e-05)[:, None] * gain[None, :]).astype(jnp.bfloat16)
    whole = lax.all_gather(xn, "tp", axis=1, tiled=True)
    empty = (
        jnp.zeros((rows, q_cols), jnp.float32),
        jnp.zeros((rows, kv_cols), jnp.float32),
        jnp.zeros((rows, kv_cols), jnp.float32),
    )
    pieces = (
        lax.all_gather(q_weight[0], "ctx", axis=0, tiled=True),
        lax.all_gather(k_weight[0], "ctx", axis=0, tiled=True),
        lax.all_gather(v_weight[0], "ctx", axis=0, tiled=True),
    )

    def really(values):
        return tuple(
            (jnp.dot(whole, piece, preferred_element_type=jnp.float32) for piece in pieces)
        )

    q_sum, k_sum, v_sum = lax.cond(is_attention, really, lambda values: values, empty)
    query = q_sum.astype(jnp.bfloat16).reshape(rows, kv_local, group, head_size)
    keys = k_sum.astype(jnp.bfloat16).reshape(rows, kv_local, head_size)
    values = v_sum.astype(jnp.bfloat16).reshape(rows, kv_local, head_size)
    q_pos = first + jnp.arange(rows)
    fold, initial, finish = make_fold(query, q_pos, doc_ids, ids_all, 1, head_size, is_attention)
    carry = fold(
        initial(kv_local, group),
        (
            lax.all_gather(keys, "ctx", axis=0, tiled=True),
            lax.all_gather(values, "ctx", axis=0, tiled=True),
        ),
        jnp.int32(0),
    )
    attended = finish(carry)
    attention_result = (current.astype(jnp.float32) + attended.astype(jnp.float32)).astype(
        jnp.bfloat16
    )
    ssm_local = dt_bias.shape[1]
    channels = width // ssm_local
    inputs = xn.astype(jnp.float32).reshape(rows, ssm_local, channels)
    maps, step_all = lax.psum(
        (
            jnp.dot(xn, bc_weight[0], preferred_element_type=jnp.float32),
            jnp.dot(xn, dt_weight[0], preferred_element_type=jnp.float32),
        ),
        "tp",
    )
    step = jax.nn.softplus(
        lax.dynamic_slice_in_dim(step_all, tp_pos * ssm_local, ssm_local, 1) + dt_bias[0][None, :]
    )
    state_size = maps.shape[1] // 2
    in_map = maps[:, :state_size]
    out_map = maps[:, state_size:]
    cumulative = jnp.cumsum(-step * decay_rate[0][None, :], axis=0)
    order = jnp.arange(rows)
    pairs = (doc_ids[:, None] == doc_ids[None, :]) & (order[:, None] >= order[None, :])
    exponent = jnp.where(
        pairs[:, :, None], cumulative[:, None, :] - cumulative[None, :, :], -jnp.inf
    )
    intersection = jnp.dot(out_map, in_map.T, precision=lax.Precision.HIGHEST)
    weighted = inputs * step[:, :, None]
    inner = jnp.einsum(
        "tsh,shp->thp",
        jnp.exp(exponent) * intersection[:, :, None],
        weighted,
        precision=lax.Precision.HIGHEST,
    )
    end_weight = (
        jnp.exp(cumulative[-1][None, :] - cumulative)
        * (doc_ids == doc_ids[-1]).astype(jnp.float32)[:, None]
    )
    end_state = jnp.einsum(
        "sh,sn,shp->hnp", end_weight, in_map, weighted, precision=lax.Precision.HIGHEST
    )
    total_decay = jnp.exp(cumulative[-1]) * (doc_ids[-1] == prev_id).astype(jnp.float32)

    def combine(earlier, later):
        return (earlier[0] * later[0], earlier[1] * later[0][:, None, None] + later[1])

    identity = (jnp.ones_like(total_decay), jnp.zeros_like(end_state))
    incoming = entering((total_decay, end_state), "ctx", combine, identity)[1]
    reach = jnp.exp(cumulative) * (doc_ids == prev_id).astype(jnp.float32)[:, None]
    carried = (
        jnp.einsum("tn,hnp->thp", out_map, incoming, precision=lax.Precision.HIGHEST)
        * reach[:, :, None]
    )
    outputs = inner + carried + skip_gain[0][None, :, None] * inputs
    outputs = outputs * lax.rsqrt(jnp.mean(outputs * outputs, axis=2, keepdims=True) + 1e-05)
    state_result = (current.astype(jnp.float32) + outputs.reshape(rows, width)).astype(jnp.bfloat16)
    produced = jnp.where(is_attention, attention_result, state_result)
    moved = passed_along(produced, "pipe", 1)
    return (produced[None], moved[None])


def solution(mesh):
    in_specs = (
        P("pipe", "ctx", "tp"),
        P("ctx"),
        P("pipe"),
        P("pipe", "tp"),
        P("pipe", "ctx", "tp"),
        P("pipe", "ctx", "tp"),
        P("pipe", "ctx", "tp"),
        P("pipe", "tp", None),
        P("pipe", "tp", None),
        P("pipe", "tp"),
        P("pipe", "tp"),
        P("pipe", "tp"),
    )
    out_specs = (P("pipe", "ctx", "tp"), P("pipe", "ctx", "tp"))
    return jax.shard_map(shards, mesh=mesh, in_specs=in_specs, out_specs=out_specs, check_vma=False)
```

profile of v0, /device:TPU:1, one launch (start us, length us, event | category | flops | bytes accessed | tf_op | source)
XLA Modules:
  0.0 225.3 jit_solution(4405542726115221422)
XLA Ops:
  7.3 0.7 all-gather.15.cloned.1.call-update
  8.0 0.7 all-gather.17.cloned.1.call-update
  8.7 1.1 fusion.28
  9.8 10.8 %psum.21 = f32[128]{0:T(128)S(1)} all-reduce(f32[128]{0:T(128)S(1)} %fusion.28), channel_id=1, replica_groups=mesh['pipe'=4,'ctx'=2,'tp'=4] {'tp'}, use_global_device_ids=true, to_apply=%region_2.3 | all-reduce | flops 128 | bytes 1024 | tf_op jit(solution)/shard_map/psum | solution.py:142
  20.6 1.8 fusion.30
  22.5 0.5 all-gather.19.cloned.1.call-update
  23.0 1.2 slice.17
  24.2 3.6 %all-gather.6 = s32[2,1,128]{2,1,0:T(1,128)S(1)} all-gather(s32[1,1,128]{2,1,0:T(1,128)} %bitcast.146), channel_id=1, replica_groups=mesh['pipe'=4,'ctx'=2,'tp'=4] {'ctx'}, dimensions={0}, use_global_device_ids=true | all-gather | bytes 1536 | tf_op jit(solution)/shard_map/all_gather | solution.py:126
  27.8 0.6 dynamic_slice.22
  29.6 1.2 fusion.45
  30.9 1.3 fusion.42
  32.1 12.8 %all-reduce = (f32[128,64]{0,1:T(8,128)S(1)}, f32[128,32]{0,1:T(8,128)S(1)}) all-reduce(f32[128,64]{0,1:T(8,128)S(1)} %fusion.42, f32[128,32]{0,1:T(8,128)S(1)} %fusion.45), channel_id=1, replica_groups=mesh['pipe'=4,'ctx'=2,'tp'=4] {'tp'}, use_global_device_ids=true, to_apply=%region_9.10 | all-reduce | flops 12288 | bytes 98304 | tf_op jit(solution)/shard_map/psum | solution.py:182
  44.9 0.8 negate_multiply_fusion
  45.7 0.1 copy.42
  45.8 0.2 reduce_window_sum.11
  46.0 3.5 %all-gather.7 = bf16[2,1,16]{2,1,0:T(2,128)(2,1)S(1)} all-gather(bf16[1,1,16]{2,1,0:T(2,128)(2,1)S(1)} %get-tuple-element.201), channel_id=1, replica_groups=mesh['pipe'=4,'ctx'=2,'tp'=4] {'ctx'}, dimensions={0}, use_global_device_ids=true | all-gather | bytes 96 | tf_op jit(solution)/shard_map/all_gather | solution.py:13
  49.4 0.6 fusion.58
  50.1 1.1 copy.41
  52.5 0.5 broadcast.209
  53.0 0.7 reduce.6
  53.7 0.1 mul.178
  53.8 0.6 compare_convert_fusion
  54.4 0.1 exponential_multiply_fusion.1
  54.5 0.1 copy.45
  54.6 1.0 convolution_convert_fusion.1
  55.6 3.8 %all-gather.5 = bf16[32,16,64]{2,1,0:T(8,128)(2,1)S(1)} all-gather(bf16[16,16,64]{2,1,0:T(8,128)(2,1)S(1)} %convolution_convert_fusion.1), channel_id=7, replica_groups=mesh['pipe'=4,'ctx'=2,'tp'=4] {'ctx'}, dimensions={0}, use_global_device_ids=true | all-gather | bytes 98304 | tf_op jit(solution)/shard_map/all_gather | solution.py:13
  59.4 0.1 fusion.51
  59.5 0.3 fusion.54
  59.8 0.3 while.14
  59.8 0.1 fusion.71
  60.0 0.1 fusion.71
  60.1 1.0 convolution_multiply_fusion.1
  61.1 2.3 %multiply_reduce_fusion = (f32[128,16]{0,1:T(8,128)S(1)}, f32[128,16,64]{0,2,1:T(8,128)S(1)}) fusion(f32[16,64]{1,0:T(8,128)S(1)} %mul.178, f32[128,16,64]{0,2,1:T(8,128)S(1)} %bitcast.139, f32[128]{0:T(128)S(1)} %add_rsqrt_fusion.1, f32[16]{0:T(128)S(1)} %bitcast.151, f32[128,16,64]{0,2,1:T(8,128)S(1)} %convolution_multiply_fusion.1, ...), kind=kOutput, calls=%fused_computation.54 | convolution fusion | flops 203945984 | bytes 1684032 | tf_op jit(solution)/shard_map/tsh,shp->thp/dot_general | solution.py:203
  63.5 0.2 copy.47
  63.7 0.2 copy.49
  63.9 22.0 %all-gather.13.cloned.1.call-done = bf16[128,4096]{1,0:T(8,128)(2,1)} async-done(((bf16[128,1024]{1,0:T(8,128)(2,1)}), bf16[128,4096]{1,0:T(8,128)(2,1)}) %all-gather.13.cloned.1.call-update) | async-done | bytes 1048592 | tf_op jit(solution)/shard_map/all_gather | solution.py:144
  85.9 105.1 %all-gather.19.cloned.1.call-done = bf16[1,4096,1024]{2,1,0:T(8,128)(2,1)} async-done(((bf16[1,2048,1024]{2,1,0:T(8,128)(2,1)}), bf16[1,4096,1024]{2,1,0:T(8,128)(2,1)}) %all-gather.19.cloned.1.call-update) | async-done | bytes 8388624 | tf_op jit(solution)/shard_map/all_gather | solution.py:151
  191.0 0.1 conditional.2
  191.1 3.4 %all-gather.3 = bf16[256,128]{1,0:T(8,128)(2,1)S(1)} all-gather(bf16[128,128]{1,0:T(8,128)(2,1)S(1)} %get-tuple-element.135), channel_id=5, replica_groups=mesh['pipe'=4,'ctx'=2,'tp'=4] {'ctx'}, dimensions={0}, use_global_device_ids=true | all-gather | bytes 98304 | tf_op jit(solution)/shard_map/all_gather | solution.py:170
  194.5 3.4 %all-gather.4 = bf16[256,128]{1,0:T(8,128)(2,1)S(1)} all-gather(bf16[128,128]{1,0:T(8,128)(2,1)S(1)} %get-tuple-element.137), channel_id=6, replica_groups=mesh['pipe'=4,'ctx'=2,'tp'=4] {'ctx'}, dimensions={0}, use_global_device_ids=true | all-gather | bytes 98304 | tf_op jit(solution)/shard_map/all_gather | solution.py:171
  198.0 0.2 convert_bitcast_fusion
  198.2 0.3 copy.40
  198.5 0.1 reshape.309
  198.6 0.2 fusion.37
  198.8 15.9 %collective-permute-start = (bf16[128,1024]{1,0:T(8,128)(2,1)S(1)}, bf16[128,1024]{1,0:T(8,128)(2,1)S(1)}, u32[]{:S(2)}, u32[]{:S(2)}) collective-permute-start(bf16[128,1024]{1,0:T(8,128)(2,1)S(1)} %fusion.37), channel_id=1, source_target_pairs={{0,8},{8,16},{16,24},{1,9},{9,17},{17,25},{2,10},{10,18},{18,26},{... | collective-permute-start | bytes 786440 | tf_op jit(solution)/shard_map/ppermute | solution.py:32
  214.8 0.8 fusion.38
  215.6 2.5 %collective-permute-done = bf16[128,1024]{1,0:T(8,128)(2,1)S(1)} collective-permute-done((bf16[128,1024]{1,0:T(8,128)(2,1)S(1)}, bf16[128,1024]{1,0:T(8,128)(2,1)S(1)}, u32[]{:S(2)}, u32[]{:S(2)}) %collective-permute-start) | collective-permute-done | bytes 262176 | tf_op jit(solution)/shard_map/ppermute | solution.py:32
  218.1 0.7 copy.83
  (37 shorter events, 0.6 us)
Async XLA Ops:
  7.2 23.7 %copy-start = (bf16[1,1024,64]{1,2,0:T(8,128)(2,1)S(1)}, bf16[1,1024,64]{1,2,0:T(8,128)(2,1)}, u32[]{:S(2)}) copy-start(bf16[1,1024,64]{1,2,0:T(8,128)(2,1)} %param.26) | copy-start | bytes 393220
  7.2 45.9 %copy-start.2 = (f32[1,1024]{1,0:T(1,128)S(1)}, f32[1,1024]{1,0:T(1,128)}, u32[]{:S(2)}) copy-start(f32[1,1024]{1,0:T(1,128)} %param.21) | copy-start | bytes 12292
  7.2 46.6 %copy-start.3 = (s32[128]{0:T(128)S(1)}, s32[128]{0:T(128)}, u32[]{:S(2)}) copy-start(s32[128]{0:T(128)} %param.19) | copy-start | bytes 1540
  7.2 53.9 %copy-start.4 = (f32[1,16]{1,0:T(1,128)S(1)}, f32[1,16]{1,0:T(1,128)}, u32[]{:S(2)}) copy-start(f32[1,16]{1,0:T(1,128)} %param.29) | copy-start | bytes 196
  7.2 56.7 %all-gather.15.cloned.1.call-start = ((), (), s32[]{:S(2)}) async-start(), calls=%async_computation.1 | async-start | bytes 1572864 | tf_op jit(solution)/shard_map/all_gather | solution.py:152
  7.9 56.0 %all-gather.17.cloned.1.call-start = ((), (), s32[]{:S(2)}) async-start(), calls=%async_computation.2 | async-start | bytes 1572864 | tf_op jit(solution)/shard_map/all_gather | solution.py:153
  8.7 77.2 %all-gather.13.cloned.1.call-start = ((), (), s32[]{:S(2)}) async-start(), calls=%async_computation | async-start | bytes 1310720 | tf_op jit(solution)/shard_map/all_gather | solution.py:144
  22.4 168.6 %all-gather.19.cloned.1.call-start = ((), (), s32[]{:S(2)}) async-start(), calls=%async_computation.3 | async-start | bytes 12582912 | tf_op jit(solution)/shard_map/all_gather | solution.py:151
  191.0 7.6 %copy-start.1 = (bf16[1,128,1024]{2,1,0:T(8,128)(2,1)S(1)}, bf16[1,128,1024]{2,1,0:T(8,128)(2,1)}, u32[]{:S(2)}) copy-start(bf16[1,128,1024]{2,1,0:T(8,128)(2,1)} %param.18) | copy-start | bytes 786436
  198.8 19.3 %collective-permute-start = (bf16[128,1024]{1,0:T(8,128)(2,1)S(1)}, bf16[128,1024]{1,0:T(8,128)(2,1)S(1)}, u32[]{:S(2)}, u32[]{:S(2)}) collective-permute-start(bf16[128,1024]{1,0:T(8,128)(2,1)S(1)} %fusion.37), channel_id=1, source_target_pairs={{0,8},{8,16},{16,24},{1,9},{9,17},{17,25},{2,10},{10,18},{18,26},{... | collective-permute-start | bytes 786440 | tf_op jit(solution)/shard_map/ppermute | solution.py:32
Sparse Core Ops, SparseCore 0:
  9.6 23.3 all-gather.14
  34.6 21.3 all-gather.16
  58.1 27.7 all-gather.12
  87.3 103.6 all-gather.18
where the time goes:
time: 223 us; the launch traced here: 225 us
  waiting for transfers between devices  131 us (59%)
  blocking collectives  41.3 us (19%)
  between operations  16.6 us (7%)
  starting transfers between devices  16.1 us (7%)
  other arithmetic  7.33 us (3%)
  matrix products  7.12 us (3%)
  local copies, waits for them, and re-layouts  5.37 us (2%)
    all_gather x1, waiting for transfers between devices, shards(): lax.all_gather(q_weight[0], 'ctx', axis=0, tiled=True)  105 us
    all_gather x1, waiting for transfers between devices, shards(): whole = lax.all_gather(xn, 'tp', axis=1, tiled=True)  22 us
    ppermute x1, starting transfers between devices, passed_along(): return lax.ppermute(x, axis, pairs)  15.9 us
    psum x1, blocking collectives, shards(): lax.psum((jnp.dot(xn, bc_weight[0], preferred_element_type=jnp.float32),...  12.8 us
    psum x1, blocking collectives, shards(): squares = lax.psum(jnp.sum(hf * hf, axis=1), 'tp')  10.8 us
    all_gather x2, blocking collectives, entering(): lax.all_gather(part.astype(kind), axis)  7.26 us
  transfers between devices with their start and end apart: 5, of which 3 were waited for; matrix products, arithmetic and copies ran while one was open for 8% of the time, Pallas kernels for 0%

commit v1 on v0

--- a/solution.py
+++ b/solution.py
@@ -1,6 +1,8 @@
 import jax
 import jax.numpy as jnp
 from jax import lax
+from jax.experimental import pallas as pl
+from jax.experimental.pallas import tpu as pltpu
 from jax.sharding import PartitionSpec as P
 
 D = 4096
@@ -233,6 +235,607 @@
     return (produced[None], moved[None])
 
 
+CHUNKS = 2
+MESH = pl.DeviceIdType.MESH
+F32 = jnp.float32
+BF16 = jnp.bfloat16
+
+
+def dot(a, b):
+    return jnp.dot(a, b, preferred_element_type=F32)
+
+
+def exact(a, b):
+    return jnp.dot(a, b, preferred_element_type=F32, precision=lax.Precision.HIGHEST)
+
+
+def column_of(row, count):
+    same = lax.broadcasted_iota(jnp.int32, (count, count), 0) == lax.broadcasted_iota(
+        jnp.int32, (count, count), 1
+    )
+    return jnp.sum(jnp.where(same, row, 0.0), axis=1, keepdims=True)
+
+
+def kernel(
+    h_ref,
+    ids_ref,
+    kind_ref,
+    gain_ref,
+    q_hbm,
+    k_hbm,
+    v_hbm,
+    bc_ref,
+    dt_ref,
+    bias_ref,
+    rate_ref,
+    skip_ref,
+    out_ref,
+    passed_ref,
+    blocks,
+    wq,
+    wkv,
+    xn_ref,
+    squares_out,
+    squares_in,
+    sums_out,
+    sums_in,
+    info_out,
+    info_in,
+    state_out,
+    state_in,
+    part_out,
+    part_in,
+    kvpart_out,
+    kvpart_in,
+    own_q,
+    own_kv,
+    kv_all,
+    q_all,
+    state_res,
+    cols_ref,
+    rows_ref,
+    direct_ref,
+    gram_ref,
+    prod,
+    prev,
+    w_sem,
+    right_sem,
+    left_sem,
+    across_sem,
+    z_recv,
+    x_recv,
+    squares_ssem,
+    squares_rsem,
+    sums_ssem,
+    sums_rsem,
+    small_ssem,
+    small_rsem,
+    part_ssem,
+    part_rsem,
+    pipe_ssem,
+    pipe_rsem,
+):
+    p, c, t = lax.axis_index("pipe"), lax.axis_index("ctx"), lax.axis_index("tp")
+    pipes, tps = lax.axis_size("pipe"), lax.axis_size("tp")
+    oc = 1 - c
+    rows, width = h_ref.shape
+    step_rows = rows // CHUNKS
+    heads = bias_ref.shape[1]
+    pairs = heads // 2
+    channels = width // heads
+    n_state = bc_ref.shape[1] // 2
+    half = tps // 2
+    q_cols = wq.shape[1]
+    q_heads = q_cols // HD
+
+    loads = [
+        pltpu.make_async_copy(q_hbm, wq, w_sem.at[0]),
+        pltpu.make_async_copy(k_hbm, wkv.at[0], w_sem.at[1]),
+        pltpu.make_async_copy(v_hbm, wkv.at[1], w_sem.at[2]),
+    ]
+    for load in loads:
+        load.start()
+
+    barrier = pltpu.get_barrier_semaphore()
+    for other in range(1, tps):
+        pl.semaphore_signal(
+            barrier, inc=1, device_id={"tp": lax.rem(t + other, tps)}, device_id_type=MESH
+        )
+    pl.semaphore_signal(barrier, inc=1, device_id={"ctx": oc}, device_id_type=MESH)
+
+    @pl.when(p > 0)
+    def _():
+        pl.semaphore_signal(barrier, inc=1, device_id={"pipe": p - 1}, device_id_type=MESH)
+
+    @pl.when(p < pipes - 1)
+    def _():
+        pl.semaphore_signal(barrier, inc=1, device_id={"pipe": p + 1}, device_id_type=MESH)
+
+    hf = h_ref[...].astype(F32)
+    gain = gain_ref[...]
+    hg = (hf * gain).astype(BF16)
+    blocks[c, t] = hg
+    squares = jnp.sum(hf * hf, axis=1, keepdims=True)
+    squares_out[...] = jnp.broadcast_to(squares, (rows, 128)).T[0:8]
+    squares_in[t] = squares_out[...]
+
+    neighbours = (p > 0).astype(jnp.int32) + (p < pipes - 1).astype(jnp.int32)
+    pl.semaphore_wait(barrier, tps + neighbours)
+
+    def span(ch):
+        return pl.ds(ch * step_rows, step_rows)
+
+    def to_tp(b, ch, target, sem):
+        ref = blocks.at[c, b, span(ch)]
+        return pltpu.make_async_remote_copy(
+            ref, ref, sem, z_recv.at[b, ch], device_id={"tp": target}, device_id_type=MESH
+        )
+
+    def to_ctx(b, ch):
+        ref = blocks.at[c, b, span(ch)]
+        j = lax.rem(b, half)
+        return pltpu.make_async_remote_copy(
+            ref,
+            ref,
+            across_sem.at[j, ch],
+            x_recv.at[j, ch],
+            device_id={"ctx": oc},
+            device_id_type=MESH,
+        )
+
+    def send_right(d, ch, go=True):
+        @pl.when((t - d >= 0) & (t < tps - 1))
+        def _():
+            copy = to_tp(t - d, ch, t + 1, right_sem.at[d, ch])
+            copy.start() if go else copy.wait_send()
+
+    def send_left(d, ch, go=True):
+        @pl.when((t + d < tps) & (t > 0))
+        def _():
+            copy = to_tp(t + d, ch, t - 1, left_sem.at[d, ch])
+            copy.start() if go else copy.wait_send()
+
+    def send_across(b, ch):
+        @pl.when((b >= 0) & (b < tps) & (b // half == oc))
+        def _():
+            to_ctx(b, ch).start()
+
+    def own_sends(ch):
+        send_right(0, ch)
+        send_left(0, ch)
+        send_across(t, ch)
+
+    def forward(d, ch):
+        @pl.when(t - d >= 0)
+        def _():
+            to_tp(t - d, ch, t, right_sem.at[0, ch]).wait_recv()
+
+        send_right(d, ch)
+        send_across(t - d, ch)
+
+        @pl.when(t + d < tps)
+        def _():
+            to_tp(t + d, ch, t, left_sem.at[0, ch]).wait_recv()
+
+        send_left(d, ch)
+        send_across(t + d, ch)
+
+    def gathered(out, into, ssem, rsem, k, mine):
+        source = out.at[k] if len(out.shape) == 3 else out
+        place = t if mine else k
+        return pltpu.make_async_remote_copy(
+            source,
+            into.at[place],
+            ssem.at[k],
+            rsem.at[place],
+            device_id={"tp": k},
+            device_id_type=MESH,
+        )
+
+    def squares_copy(k, mine):
+        return gathered(squares_out, squares_in, squares_ssem, squares_rsem, k, mine)
+
+    def sums_copy(k, mine):
+        return gathered(sums_out, sums_in, sums_ssem, sums_rsem, k, mine)
+
+    peers = [lax.rem(t + other, tps) for other in range(1, tps)]
+    for k in peers:
+        squares_copy(k, True).start()
+    own_sends(0)
+    for k in peers:
+        squares_copy(k, False).wait_recv()
+    squares = squares_in[0]
+    for k in range(1, tps):
+        squares = squares + squares_in[k]
+    r_row = lax.rsqrt(squares / D + 1e-05)
+    r_wide = jnp.broadcast_to(r_row[0:1], (128, rows)).T
+    xn = (hf * r_wide[:, 0:1] * gain).astype(BF16)
+    xn_ref[...] = xn
+    dt_at = 2 * n_state
+    packed = jnp.concatenate(
+        [
+            dot(xn, bc_ref[...]),
+            dot(xn, dt_ref[...]),
+            jnp.zeros((rows, 128 - dt_at - heads * tps), F32),
+        ],
+        axis=1,
+    ).T
+    for k in range(tps):
+        dt_row = dt_at + k * heads
+        sums_out[k] = jnp.concatenate([packed[:dt_at], packed[dt_row : dt_row + heads]], axis=0)
+    sums_in[t] = sums_out[t]
+    for k in peers:
+        sums_copy(k, True).start()
+    ids_row = ids_ref[...].astype(F32)
+    info_out[0:8] = r_row
+    info_out[8:16] = jnp.broadcast_to(ids_row, (8, rows))
+    info_copy = pltpu.make_async_remote_copy(
+        info_out,
+        info_in,
+        small_ssem.at[0],
+        small_rsem.at[0],
+        device_id={"ctx": oc},
+        device_id_type=MESH,
+    )
+    info_copy.start()
+    for ch in range(1, CHUNKS):
+        own_sends(ch)
+    for k in peers:
+        sums_copy(k, False).wait_recv()
+
+    total = sums_in[0]
+    for k in range(1, tps):
+        total = total + sums_in[k]
+    maps = total[:dt_at]
+    drive = total[dt_at : dt_at + heads] + column_of(bias_ref[...], heads)
+    step = jnp.maximum(drive, 0.0) + jnp.log1p(jnp.exp(-jnp.abs(drive)))
+    upper = (
+        lax.broadcasted_iota(jnp.int32, (rows, rows), 0)
+        <= lax.broadcasted_iota(jnp.int32, (rows, rows), 1)
+    ).astype(F32)
+    cum = exact(-step * column_of(rate_ref[...], heads), upper)
+    cols = jnp.concatenate(
+        [
+            maps,
+            cum,
+            r_row,
+            jnp.broadcast_to(ids_row, (8, rows)),
+            step,
+            jnp.zeros((128 - dt_at - 2 * heads - 16, rows), F32),
+        ],
+        axis=0,
+    ).T
+    cols_ref[...] = cols
+    r_at = dt_at + heads
+    ids_col = cols[:, r_at + 8 : r_at + 9]
+    low = lax.broadcasted_iota(jnp.int32, (rows, rows), 0) > lax.broadcasted_iota(
+        jnp.int32, (rows, rows), 1
+    )
+    allowed = (ids_col == ids_row) & low
+    gram_ref[0] = jnp.where(allowed, exact(cols[:, n_state:dt_at], maps[:n_state]), 0.0)
+    in_cols, out_cols = cols[:, :n_state], cols[:, n_state:dt_at]
+    own_term = jnp.sum(in_cols * out_cols, axis=1, keepdims=True)
+    direct_ref[...] = cols[:, r_at + 16 : r_at + 16 + heads] * own_term + skip_ref[...]
+    gram_ref[1] = jnp.where(allowed, 0.0, -1e30)
+    rows_ref[0:heads] = cum
+    rows_ref[heads : 2 * heads] = step
+    tail = (
+        jnp.exp(cum[:, rows - 1 : rows] - cum)
+        * jnp.where(ids_row == ids_row[:, rows - 1 : rows], 1.0, 0.0)
+        * step
+    )
+    left_lanes = lax.broadcasted_iota(jnp.int32, (1, 2 * channels), 1) < channels
+    for i in range(pairs):
+        x_pair = xn_ref[:, i * 2 * channels : (i + 1) * 2 * channels]
+        weights = jnp.concatenate(
+            [maps[:n_state] * tail[2 * i + k : 2 * i + k + 1] for k in range(2)], axis=0
+        ).astype(BF16)
+        ends = dot(weights, x_pair)
+        state_out[i] = jnp.where(left_lanes, ends[:n_state], ends[n_state:]).astype(BF16)
+    state_copy = pltpu.make_async_remote_copy(
+        state_out,
+        state_in,
+        small_ssem.at[1],
+        small_rsem.at[1],
+        device_id={"ctx": oc},
+        device_id_type=MESH,
+    )
+    state_copy.start()
+
+    def state_pair(i):
+        x_pair = xn_ref[:, i * 2 * channels : (i + 1) * 2 * channels]
+        outs, decays = [], []
+        reach = jnp.where(
+            (cols_ref[:, r_at + 8 : r_at + 9] == info_in[8:9, rows - 1 : rows]) & (c > 0), 1.0, 0.0
+        )
+        for head in (2 * i, 2 * i + 1):
+            cum_col = cols_ref[:, dt_at + head : dt_at + head + 1]
+            decay = jnp.exp(cum_col - rows_ref[head : head + 1] + gram_ref[1])
+            mixed = decay * gram_ref[0] * rows_ref[heads + head : heads + head + 1]
+            outs.append(dot(mixed.astype(BF16), x_pair))
+            decays.append(jnp.exp(cum_col) * reach)
+        skips = [direct_ref[:, 2 * i + k : 2 * i + k + 1] for k in range(2)]
+        carried = dot(cols_ref[:, n_state:dt_at].astype(BF16), state_in[i])
+        y = (
+            jnp.where(left_lanes, outs[0], outs[1])
+            + carried * jnp.where(left_lanes, decays[0], decays[1])
+            + jnp.where(left_lanes, skips[0], skips[1]) * x_pair.astype(F32)
+        )
+        squared = y * y
+        first = jnp.sum(jnp.where(left_lanes, squared, 0.0), axis=1, keepdims=True)
+        second = jnp.sum(jnp.where(left_lanes, 0.0, squared), axis=1, keepdims=True)
+        mean = jnp.where(left_lanes, first, second) / channels
+        z = y * lax.rsqrt(mean + 1e-05)
+        lanes = slice(i * 2 * channels, (i + 1) * 2 * channels)
+        state_res[:, lanes] = (h_ref[:, lanes].astype(F32) + z).astype(BF16)
+
+    def project(tok, ch, column):
+        total = None
+        for j in range(half):
+            x = blocks[tok, half * c + j, span(ch)]
+            depth = slice(j * width, (j + 1) * width)
+            if column < q_cols:
+                w = wq[depth, column : column + 256]
+            else:
+                w = jnp.concatenate([wkv[0, depth], wkv[1, depth]], axis=1)
+            term = dot(x, w)
+            total = term if total is None else total + term
+        return total
+
+    def part_copy(ch):
+        return pltpu.make_async_remote_copy(
+            part_out.at[span(ch)],
+            part_in.at[span(ch)],
+            part_ssem.at[0, ch],
+            part_rsem.at[0, ch],
+            device_id={"ctx": oc},
+            device_id_type=MESH,
+        )
+
+    def kvpart_copy(ch):
+        return pltpu.make_async_remote_copy(
+            kvpart_out.at[span(ch)],
+            kvpart_in.at[span(ch)],
+            part_ssem.at[1, ch],
+            part_rsem.at[1, ch],
+            device_id={"ctx": oc},
+            device_id_type=MESH,
+        )
+
+    def x_arrival(j, ch):
+        ref = blocks.at[oc, half * c + j, span(ch)]
+        return pltpu.make_async_remote_copy(
+            ref,
+            ref,
+            across_sem.at[j, ch],
+            x_recv.at[j, ch],
+            device_id={"ctx": oc},
+            device_id_type=MESH,
+        )
+
+    def project_theirs(ch):
+        for j in range(half):
+            x_arrival(j, ch).wait_recv()
+        for column in range(0, q_cols + 256, 256):
+            value = project(oc, ch, column)
+            part_out[span(ch), column : column + 256] = value.astype(BF16)
+            if column == q_cols:
+                own_kv[oc, span(ch)] = value
+        part_copy(ch).start()
+
+    def project_ours(ch):
+        value = project(c, ch, q_cols)
+        own_kv[c, span(ch)] = value
+        kvpart_out[span(ch)] = value.astype(BF16)
+        kvpart_copy(ch).start()
+        for column in range(0, q_cols, 256):
+            own_q[span(ch), column : column + 256] = project(c, ch, column)
+
+    done = 0
+    steps = [(ch, d) for ch in range(CHUNKS) for d in range(1, tps)]
+    for n, (ch, d) in enumerate(steps):
+        forward(d, ch)
+        if n == 0:
+            info_copy.wait_recv()
+            state_copy.wait_recv()
+            for load in loads:
+                load.wait()
+        upto = pairs * (n + 1) // len(steps)
+        for i in range(done, upto):
+            state_pair(i)
+        done = upto
+        if d == tps - 1:
+            project_theirs(ch)
+            project_ours(ch)
+
+    r_col = cols_ref[:, r_at : r_at + 1]
+    their_r = jnp.broadcast_to(info_in[0:1], (128, rows)).T[:, 0:1]
+    for ch in range(CHUNKS):
+        part_copy(ch).wait_recv()
+        kvpart_copy(ch).wait_recv()
+    q_all[...] = ((own_q[...] + part_in[:, :q_cols].astype(F32)) * r_col).astype(BF16)
+    kv_all[c] = ((own_kv[c] + part_in[:, q_cols:].astype(F32)) * r_col).astype(BF16)
+    kv_all[oc] = ((own_kv[oc] + kvpart_in[...].astype(F32)) * their_r).astype(BF16)
+
+    key_pos = lax.broadcasted_iota(jnp.int32, (rows, 2 * rows), 1)
+    query_pos = c * rows + lax.broadcasted_iota(jnp.int32, (rows, 2 * rows), 0)
+    my_ids, their_ids = ids_row, info_in[8:9]
+    at_first = jnp.where(c == 0, my_ids, their_ids)
+    at_second = jnp.where(c == 0, their_ids, my_ids)
+    key_ids = jnp.concatenate([at_first, at_second], axis=1)
+    wanted = (key_pos <= query_pos) & (key_ids == cols_ref[:, r_at + 8 : r_at + 9])
+    keys = kv_all[:, :, :HD].reshape(2 * rows, HD)
+    values = kv_all[:, :, HD:].reshape(2 * rows, HD)
+    attention = kind_ref[...] == 1
+    per = prod.shape[2] // HD
+
+    def pipe_copy(k):
+        return pltpu.make_async_remote_copy(
+            prod.at[k],
+            prev.at[k],
+            pipe_ssem.at[k],
+            pipe_rsem.at[k],
+            device_id={"pipe": p + 1},
+            device_id_type=MESH,
+        )
+
+    for head in range(q_heads):
+        lanes = slice(head * HD, (head + 1) * HD)
+        scores = lax.dot_general(
+            q_all[:, lanes], keys, (((1,), (1,)), ((), ())), preferred_element_type=F32
+        ) * (HD ** (-0.5))
+        scores = jnp.where(wanted, scores, -1e30)
+        top = jnp.max(scores, axis=1, keepdims=True)
+        probs = jnp.where(wanted, jnp.exp(scores - top), 0.0)
+        denom = jnp.sum(probs, axis=1, keepdims=True)
+        mixed = (dot(probs.astype(BF16), values) / denom).astype(BF16)
+        attended = (h_ref[:, lanes].astype(F32) + mixed.astype(F32)).astype(BF16)
+        result = jnp.where(
+            jnp.broadcast_to(attention, (rows, HD)),
+            attended.astype(F32),
+            state_res[:, lanes].astype(F32),
+        ).astype(BF16)
+        out_ref[:, lanes] = result
+        inner = head % per
+        prod[head // per, :, inner * HD : (inner + 1) * HD] = result
+        if inner == per - 1:
+
+            @pl.when(p < pipes - 1)
+            def _(k=head // per):
+                pipe_copy(k).start()
+
+    for ch in range(CHUNKS):
+        for d in range(tps):
+            send_right(d, ch, False)
+            send_left(d, ch, False)
+        for j in range(half):
+            to_ctx(half * oc + j, ch).wait_send()
+        part_copy(ch).wait_send()
+        kvpart_copy(ch).wait_send()
+    for k in peers:
+        squares_copy(k, True).wait_send()
+        sums_copy(k, True).wait_send()
+    info_copy.wait_send()
+    state_copy.wait_send()
+
+    span_p = prod.shape[2]
+
+    @pl.when(p > 0)
+    def _():
+        for k in range(q_heads // per):
+            pipe_copy(k).wait_recv()
+            passed_ref[:, k * span_p : (k + 1) * span_p] = prev[k]
+
+    @pl.when(p == 0)
+    def _():
+        passed_ref[...] = jnp.zeros(passed_ref.shape, BF16)
+
+    @pl.when(p < pipes - 1)
+    def _():
+        for k in range(q_heads // per):
+            pipe_copy(k).wait_send()
+
+
+def fused(
+    hidden_in,
+    doc_ids,
+    layer_kind,
+    norm_gain,
+    q_weight,
+    k_weight,
+    v_weight,
+    bc_weight,
+    dt_weight,
+    dt_bias,
+    decay_rate,
+    skip_gain,
+):
+    _, rows, width = hidden_in.shape
+    depth, q_cols = q_weight.shape[1:]
+    kv_cols = k_weight.shape[2]
+    heads = dt_bias.shape[1]
+    n_state = bc_weight.shape[2] // 2
+    tps = lax.axis_size("tp")
+    vmem = pl.BlockSpec(memory_space=pltpu.VMEM)
+    anywhere = pl.BlockSpec(memory_space=pl.ANY)
+    small = 2 * n_state + heads
+    dma = pltpu.SemaphoreType.DMA
+    shape = jax.ShapeDtypeStruct((rows, width), BF16)
+    out, passed = pl.pallas_call(
+        kernel,
+        out_shape=(shape, shape),
+        in_specs=[vmem] * 4 + [anywhere] * 3 + [vmem] * 5,
+        out_specs=(vmem, vmem),
+        scratch_shapes=[
+            pltpu.VMEM((2, tps, rows, width), BF16),
+            pltpu.VMEM((depth, q_cols), BF16),
+            pltpu.VMEM((2, depth, kv_cols), BF16),
+            pltpu.VMEM((rows, width), BF16),
+            pltpu.VMEM((8, rows), F32),
+            pltpu.VMEM((tps, 8, rows), F32),
+            pltpu.VMEM((tps, small, rows), F32),
+            pltpu.VMEM((tps, small, rows), F32),
+            pltpu.VMEM((16, rows), F32),
+            pltpu.VMEM((16, rows), F32),
+            pltpu.VMEM((heads // 2, n_state, 2 * width // heads), BF16),
+            pltpu.VMEM((heads // 2, n_state, 2 * width // heads), BF16),
+            pltpu.VMEM((rows, q_cols + 2 * kv_cols), BF16),
+            pltpu.VMEM((rows, q_cols + 2 * kv_cols), BF16),
+            pltpu.VMEM((rows, 2 * kv_cols), BF16),
+            pltpu.VMEM((rows, 2 * kv_cols), BF16),
+            pltpu.VMEM((rows, q_cols), F32),
+            pltpu.VMEM((2, rows, 2 * kv_cols), F32),
+            pltpu.VMEM((2, rows, 2 * kv_cols), BF16),
+            pltpu.VMEM((rows, q_cols), BF16),
+            pltpu.VMEM((rows, width), BF16),
+            pltpu.VMEM((rows, 128), F32),
+            pltpu.VMEM((2 * heads, rows), F32),
+            pltpu.VMEM((rows, heads), F32),
+            pltpu.VMEM((2, rows, rows), F32),
+            pltpu.VMEM((4, rows, width // 4), BF16),
+            pltpu.VMEM((4, rows, width // 4), BF16),
+            dma((3,)),
+            dma((tps, CHUNKS)),
+            dma((tps, CHUNKS)),
+            dma((tps // 2, CHUNKS)),
+            dma((tps, CHUNKS)),
+            dma((tps // 2, CHUNKS)),
+            dma((tps,)),
+            dma((tps,)),
+            dma((tps,)),
+            dma((tps,)),
+            dma((2,)),
+            dma((2,)),
+            dma((2, CHUNKS)),
+            dma((2, CHUNKS)),
+            dma((4,)),
+            dma((4,)),
+        ],
+        compiler_params=pltpu.CompilerParams(
+            collective_id=0, has_side_effects=True, vmem_limit_bytes=40 * 2**20
+        ),
+        cost_estimate=pl.CostEstimate(
+            flops=4 * rows * depth * (q_cols + 2 * kv_cols),
+            bytes_accessed=2 * depth * (q_cols + 2 * kv_cols),
+            transcendentals=0,
+        ),
+    )(
+        hidden_in[0],
+        doc_ids[None],
+        layer_kind[None],
+        norm_gain,
+        q_weight[0],
+        k_weight[0],
+        v_weight[0],
+        bc_weight[0],
+        dt_weight[0],
+        dt_bias,
+        decay_rate,
+        skip_gain,
+    )
+    return out[None], passed[None]
+
+
 def solution(mesh):
     in_specs = (
         P("pipe", "ctx", "tp"),
@@ -249,4 +852,5 @@
         P("pipe", "tp"),
     )
     out_specs = (P("pipe", "ctx", "tp"), P("pipe", "ctx", "tp"))
-    return jax.shard_map(shards, mesh=mesh, in_specs=in_specs, out_specs=out_specs, check_vma=False)
+    body = fused if mesh.shape["ctx"] == 2 and mesh.shape["tp"] == 4 else shards
+    return jax.shard_map(body, mesh=mesh, in_specs=in_specs, out_specs=out_specs, check_vma=False)

time: 223 us -> 61.3 us (0.27); the launches traced: 225 us -> 60.8 us
  waiting for transfers between devices: 131 us -> 0 us
  Pallas kernels: 0 us -> 47.5 us
  blocking collectives: 41.3 us -> 0 us
  starting transfers between devices: 16.1 us -> 0 us
  between operations: 16.6 us -> 1.32 us
  other arithmetic: 7.33 us -> 0 us
  matrix products: 7.12 us -> 0 us
  local copies, waits for them, and re-layouts: 5.37 us -> 12 us
    all_gather x4 -> x0, waiting for transfers between devices: 127 us -> none  [the longest x1 105 us: shards(): lax.all_gather(q_weight[0], 'ctx', axis=0, tiled=True)]
    pallas_call x0 -> x1, Pallas kernels: none -> 47.5 us  [fused(): pl.pallas_call(kernel, out_shape=(shape, shape), in_specs=[vmem] * 4 + [a...]
    psum x2 -> x0, blocking collectives: 23.5 us -> none  [the longest x1 12.8 us: shards(): lax.psum((jnp.dot(xn, bc_weight[0], preferred_element_type=jnp.float32),...]
    all_gather x5 -> x0, blocking collectives: 17.7 us -> none  [the longest x2 7.26 us: entering(): lax.all_gather(part.astype(kind), axis)]
    ppermute x1 -> x0, starting transfers between devices: 15.9 us -> none  [passed_along(): return lax.ppermute(x, axis, pairs)]
    unnamed x13 -> x22, local copies, waits for them, and re-layouts: 1.25 us -> 12 us
    dot_general x6 -> x0, matrix products: 7.12 us -> none  [the longest x1 2.3 us: shards(): jnp.einsum('tsh,shp->thp', jnp.exp(exponent) * intersection[:, :, None],...]
    convert_element_type x5 -> x0, other arithmetic: 2.58 us -> none  [the longest x1 1.79 us: shards(): (hf * lax.rsqrt(squares / D + 1e-05)[:, None] * gain[None, :]).astype(jnp...]
  transfers between devices with their start and end apart: 5 -> 0, of which waited for: 3 -> 0; matrix products, arithmetic and copies ran while one was open for 8% -> 0% of each run, Pallas kernels for 0% -> 0%
where the time goes in v1:
time: 61.3 us; the launch traced here: 60.8 us
  Pallas kernels  47.5 us (77%)
  local copies, waits for them, and re-layouts  12 us (20%)
  between operations  1.32 us (2%)
    pallas_call x1, Pallas kernels, fused(): pl.pallas_call(kernel, out_shape=(shape, shape), in_specs=[vmem] * 4 + [a...  47.5 us
    unnamed x22, local copies, waits for them, and re-layouts  12 us

profile of v1, /device:TPU:1, one launch (start us, length us, event | category | flops | bytes accessed | tf_op | source)
XLA Modules:
  0.0 60.8 jit_solution(87964599253527991)
XLA Ops:
  1.3 1.0 %copy.14 = bf16[1,1024,32]{2,1,0:T(8,128)(2,1)S(1)} copy(bf16[1,1024,32]{1,2,0:T(8,128)(2,1)} %param.19) | data formatting | bytes 131072 | tf_op args[7]
  2.3 1.1 %copy.15 = bf16[1,1024,64]{2,1,0:T(8,128)(2,1)S(1)} copy(bf16[1,1024,64]{1,2,0:T(8,128)(2,1)} %param.20) | data formatting | bytes 262144 | tf_op args[8]
  3.4 0.0 copy-start
  3.4 2.2 %copy-done = bf16[1,2048,1024]{2,1,0:T(8,128)(2,1)S(1)} copy-done((bf16[1,2048,1024]{2,1,0:T(8,128)(2,1)S(1)}, bf16[1,2048,1024]{2,1,0:T(8,128)(2,1)}, u32[]{:S(2)}) %copy-start) | copy-done | bytes 4194328
  5.6 0.0 copy-start.1
  5.6 1.0 %copy-done.1 = bf16[1,2048,128]{2,1,0:T(8,128)(2,1)S(1)} copy-done((bf16[1,2048,128]{2,1,0:T(8,128)(2,1)S(1)}, bf16[1,2048,128]{2,1,0:T(8,128)(2,1)}, u32[]{:S(2)}) %copy-start.1) | copy-done | bytes 524312
  6.6 0.0 copy-start.2
  6.6 1.0 %copy-done.2 = bf16[1,2048,128]{2,1,0:T(8,128)(2,1)S(1)} copy-done((bf16[1,2048,128]{2,1,0:T(8,128)(2,1)S(1)}, bf16[1,2048,128]{2,1,0:T(8,128)(2,1)}, u32[]{:S(2)}) %copy-start.2) | copy-done | bytes 524312
  7.7 0.0 copy-start.3
  7.7 0.9 %copy-done.3 = bf16[1,128,1024]{2,1,0:T(8,128)(2,1)S(1)} copy-done((bf16[1,128,1024]{2,1,0:T(8,128)(2,1)S(1)}, bf16[1,128,1024]{2,1,0:T(8,128)(2,1)}, u32[]{:S(2)}) %copy-start.3) | copy-done | bytes 262168
  8.6 0.0 copy-start.4
  8.6 0.7 %copy-done.4 = f32[1,1024]{1,0:T(1,128)S(1)} copy-done((f32[1,1024]{1,0:T(1,128)S(1)}, f32[1,1024]{1,0:T(1,128)}, u32[]{:S(2)}) %copy-start.4) | copy-done | bytes 4120
  9.3 0.0 copy-start.5
  9.3 0.7 %copy-done.5 = s32[128]{0:T(128)S(1)} copy-done((s32[128]{0:T(128)S(1)}, s32[128]{0:T(128)}, u32[]{:S(2)}) %copy-start.5) | copy-done | bytes 536
  9.9 0.0 copy-start.6
  9.9 0.7 %copy-done.6 = f32[1,16]{1,0:T(1,128)S(1)} copy-done((f32[1,16]{1,0:T(1,128)S(1)}, f32[1,16]{1,0:T(1,128)}, u32[]{:S(2)}) %copy-start.6) | copy-done | bytes 88
  10.6 0.0 copy-start.7
  10.6 0.7 %copy-done.7 = f32[1,16]{1,0:T(1,128)S(1)} copy-done((f32[1,16]{1,0:T(1,128)S(1)}, f32[1,16]{1,0:T(1,128)}, u32[]{:S(2)}) %copy-start.7) | copy-done | bytes 88
  11.3 0.0 copy-start.8
  11.3 0.7 %copy-done.8 = f32[1,16]{1,0:T(1,128)S(1)} copy-done((f32[1,16]{1,0:T(1,128)S(1)}, f32[1,16]{1,0:T(1,128)}, u32[]{:S(2)}) %copy-start.8) | copy-done | bytes 88
  11.9 47.5 %shard_map.131 = (bf16[128,1024]{1,0:T(8,128)(2,1)S(1)}, bf16[128,1024]{1,0:T(8,128)(2,1)S(1)}) custom-call(bf16[128,1024]{1,0:T(8,128)(2,1)S(1)} %bitcast.16, s32[1,128]{1,0:T(1,128)S(1)} %bitcast.19, s32[1,1]{1,0:T(1,128)} %bitcast.10.kind_ref, f32[1,1024]{1,0:T(1,128)S(1)} %copy-done.4, bf16[2048,1024]{1,0:T(8,128)(2,1)S(1)} %bitcast.11, ...), custom_call_target="tpu_custom_call" | custom-call | flops 1342177280 | bytes 5242880 | tf_op jit(solution)/shard_map/pallas_call | solution.py:764
  59.4 0.7 %copy.19 = bf16[1,128,1024]{2,1,0:T(8,128)(2,1)} copy(bf16[1,128,1024]{2,1,0:T(8,128)(2,1)S(1)} %bitcast.18) | data formatting | bytes 524288
  60.1 0.7 %copy.20 = bf16[1,128,1024]{2,1,0:T(8,128)(2,1)} copy(bf16[1,128,1024]{2,1,0:T(8,128)(2,1)S(1)} %bitcast.17) | data formatting | bytes 524288
Async XLA Ops:
  3.4 2.2 %copy-start = (bf16[1,2048,1024]{2,1,0:T(8,128)(2,1)S(1)}, bf16[1,2048,1024]{2,1,0:T(8,128)(2,1)}, u32[]{:S(2)}) copy-start(bf16[1,2048,1024]{2,1,0:T(8,128)(2,1)} %param.16) | copy-start | bytes 12582916
  5.6 1.0 %copy-start.1 = (bf16[1,2048,128]{2,1,0:T(8,128)(2,1)S(1)}, bf16[1,2048,128]{2,1,0:T(8,128)(2,1)}, u32[]{:S(2)}) copy-start(bf16[1,2048,128]{2,1,0:T(8,128)(2,1)} %param.17) | copy-start | bytes 1572868
  6.6 1.0 %copy-start.2 = (bf16[1,2048,128]{2,1,0:T(8,128)(2,1)S(1)}, bf16[1,2048,128]{2,1,0:T(8,128)(2,1)}, u32[]{:S(2)}) copy-start(bf16[1,2048,128]{2,1,0:T(8,128)(2,1)} %param.18) | copy-start | bytes 1572868
  7.7 0.9 %copy-start.3 = (bf16[1,128,1024]{2,1,0:T(8,128)(2,1)S(1)}, bf16[1,128,1024]{2,1,0:T(8,128)(2,1)}, u32[]{:S(2)}) copy-start(bf16[1,128,1024]{2,1,0:T(8,128)(2,1)} %param.12) | copy-start | bytes 786436
  8.6 0.7 %copy-start.4 = (f32[1,1024]{1,0:T(1,128)S(1)}, f32[1,1024]{1,0:T(1,128)}, u32[]{:S(2)}) copy-start(f32[1,1024]{1,0:T(1,128)} %gain_ref.1) | copy-start | bytes 12292
  9.3 0.7 %copy-start.5 = (s32[128]{0:T(128)S(1)}, s32[128]{0:T(128)}, u32[]{:S(2)}) copy-start(s32[128]{0:T(128)} %param.13) | copy-start | bytes 1540
  9.9 0.7 %copy-start.6 = (f32[1,16]{1,0:T(1,128)S(1)}, f32[1,16]{1,0:T(1,128)}, u32[]{:S(2)}) copy-start(f32[1,16]{1,0:T(1,128)} %bias_ref.1) | copy-start | bytes 196
  10.6 0.7 %copy-start.7 = (f32[1,16]{1,0:T(1,128)S(1)}, f32[1,16]{1,0:T(1,128)}, u32[]{:S(2)}) copy-start(f32[1,16]{1,0:T(1,128)} %rate_ref.1) | copy-start | bytes 196
  11.3 0.7 %copy-start.8 = (f32[1,16]{1,0:T(1,128)S(1)}, f32[1,16]{1,0:T(1,128)}, u32[]{:S(2)}) copy-start(f32[1,16]{1,0:T(1,128)} %skip_ref.1) | copy-start | bytes 196

commit v2 on v1

--- a/solution.py
+++ b/solution.py
@@ -257,23 +257,31 @@
 
 
 def kernel(
-    h_ref,
-    ids_ref,
-    kind_ref,
-    gain_ref,
+    h_hbm,
+    gain_hbm,
+    bc_hbm,
+    dt_hbm,
+    ids_hbm,
+    kind_hbm,
+    bias_hbm,
+    rate_hbm,
+    skip_hbm,
     q_hbm,
     k_hbm,
     v_hbm,
+    out_ref,
+    passed_ref,
+    h_ref,
+    gain_ref,
     bc_ref,
     dt_ref,
+    ids_ref,
+    kind_ref,
     bias_ref,
     rate_ref,
     skip_ref,
-    out_ref,
-    passed_ref,
     blocks,
-    wq,
-    wkv,
+    weight,
     xn_ref,
     squares_out,
     squares_in,
@@ -287,8 +295,7 @@
     part_in,
     kvpart_out,
     kvpart_in,
-    own_q,
-    own_kv,
+    sums_q,
     kv_all,
     q_all,
     state_res,
@@ -323,15 +330,30 @@
     heads = bias_ref.shape[1]
     pairs = heads // 2
     channels = width // heads
-    n_state = bc_ref.shape[1] // 2
+    n_state = bc_ref.shape[0] // 2
     half = tps // 2
-    q_cols = wq.shape[1]
+    q_cols = q_hbm.shape[1]
+    kv_cols = k_hbm.shape[1]
+    all_cols = q_cols + 2 * kv_cols
     q_heads = q_cols // HD
 
+    pairs_in = [
+        (h_hbm, h_ref),
+        (gain_hbm, gain_ref),
+        (bc_hbm, bc_ref),
+        (dt_hbm, dt_ref),
+        (ids_hbm, ids_ref),
+        (kind_hbm, kind_ref),
+        (bias_hbm, bias_ref),
+        (rate_hbm, rate_ref),
+        (skip_hbm, skip_ref),
+        (q_hbm, weight.at[:, pl.ds(0, q_cols)]),
+        (k_hbm, weight.at[:, pl.ds(q_cols, kv_cols)]),
+        (v_hbm, weight.at[:, pl.ds(q_cols + kv_cols, kv_cols)]),
+    ]
     loads = [
-        pltpu.make_async_copy(q_hbm, wq, w_sem.at[0]),
-        pltpu.make_async_copy(k_hbm, wkv.at[0], w_sem.at[1]),
-        pltpu.make_async_copy(v_hbm, wkv.at[1], w_sem.at[2]),
+        pltpu.make_async_copy(source, into, w_sem.at[n])
+        for n, (source, into) in enumerate(pairs_in)
     ]
     for load in loads:
         load.start()
@@ -351,6 +373,8 @@
     def _():
         pl.semaphore_signal(barrier, inc=1, device_id={"pipe": p + 1}, device_id_type=MESH)
 
+    loads[0].wait()
+    loads[1].wait()
     hf = h_ref[...].astype(F32)
     gain = gain_ref[...]
     hg = (hf * gain).astype(BF16)
@@ -452,14 +476,13 @@
     xn = (hf * r_wide[:, 0:1] * gain).astype(BF16)
     xn_ref[...] = xn
     dt_at = 2 * n_state
-    packed = jnp.concatenate(
-        [
-            dot(xn, bc_ref[...]),
-            dot(xn, dt_ref[...]),
-            jnp.zeros((rows, 128 - dt_at - heads * tps), F32),
-        ],
-        axis=1,
-    ).T
+    for load in loads[2:9]:
+        load.wait()
+
+    def against(w):
+        return lax.dot_general(w, xn, (((1,), (1,)), ((), ())), preferred_element_type=F32)
+
+    packed = jnp.concatenate([against(bc_ref[...]), against(dt_ref[...])], axis=0)
     for k in range(tps):
         dt_row = dt_at + k * heads
         sums_out[k] = jnp.concatenate([packed[:dt_at], packed[dt_row : dt_row + heads]], axis=0)
@@ -569,18 +592,16 @@
         lanes = slice(i * 2 * channels, (i + 1) * 2 * channels)
         state_res[:, lanes] = (h_ref[:, lanes].astype(F32) + z).astype(BF16)
 
-    def project(tok, ch, column):
-        total = None
-        for j in range(half):
-            x = blocks[tok, half * c + j, span(ch)]
-            depth = slice(j * width, (j + 1) * width)
-            if column < q_cols:
-                w = wq[depth, column : column + 256]
-            else:
-                w = jnp.concatenate([wkv[0, depth], wkv[1, depth]], axis=1)
-            term = dot(x, w)
-            total = term if total is None else total + term
-        return total
+    near = jnp.clip(t, half * c, half * c + half - 1) - half * c
+    far = half - 1 - near
+
+    def weight_rows(j, column):
+        return weight[pl.ds(pl.multiple_of(j * width, width), width), column : column + 256]
+
+    def project_near(tok):
+        x = blocks[tok, half * c + near]
+        for column in range(0, all_cols, 256):
+            sums_q[tok, :, column : column + 256] = dot(x, weight_rows(near, column))
 
     def part_copy(ch):
         return pltpu.make_async_remote_copy(
@@ -613,49 +634,61 @@
             device_id_type=MESH,
         )
 
-    def project_theirs(ch):
-        for j in range(half):
-            x_arrival(j, ch).wait_recv()
-        for column in range(0, q_cols + 256, 256):
-            value = project(oc, ch, column)
-            part_out[span(ch), column : column + 256] = value.astype(BF16)
-            if column == q_cols:
-                own_kv[oc, span(ch)] = value
+    def project_far(ch):
+        x_arrival(far, ch).wait_recv()
+        block = half * c + far
+        x = jnp.concatenate([blocks[oc, block, span(ch)], blocks[c, block, span(ch)]], axis=0)
+        for column in (*range(q_cols, all_cols, 256), *range(0, q_cols, 256)):
+            lanes = slice(column, column + 256)
+            value = dot(x, weight_rows(far, column))
+            theirs = value[:step_rows] + sums_q[oc, span(ch), lanes]
+            ours = value[step_rows:] + sums_q[c, span(ch), lanes]
+            part_out[span(ch), lanes] = theirs.astype(BF16)
+            sums_q[c, span(ch), lanes] = ours
+            if column >= q_cols:
+                sums_q[oc, span(ch), lanes] = theirs
+                kvpart_out[span(ch)] = ours.astype(BF16)
+                kvpart_copy(ch).start()
         part_copy(ch).start()
 
-    def project_ours(ch):
-        value = project(c, ch, q_cols)
-        own_kv[c, span(ch)] = value
-        kvpart_out[span(ch)] = value.astype(BF16)
-        kvpart_copy(ch).start()
-        for column in range(0, q_cols, 256):
-            own_q[span(ch), column : column + 256] = project(c, ch, column)
-
-    done = 0
-    steps = [(ch, d) for ch in range(CHUNKS) for d in range(1, tps)]
-    for n, (ch, d) in enumerate(steps):
-        forward(d, ch)
-        if n == 0:
-            info_copy.wait_recv()
-            state_copy.wait_recv()
-            for load in loads:
-                load.wait()
-        upto = pairs * (n + 1) // len(steps)
-        for i in range(done, upto):
-            state_pair(i)
-        done = upto
-        if d == tps - 1:
-            project_theirs(ch)
-            project_ours(ch)
+    for ch in range(CHUNKS):
+        forward(1, ch)
+    info_copy.wait_recv()
+    state_copy.wait_recv()
+    for i in range(0, pairs // 4):
+        state_pair(i)
+    for ch in range(CHUNKS):
+        forward(2, ch)
+        for i in range(pairs // 4 + ch * pairs // 4, pairs // 4 + (ch + 1) * pairs // 4):
+            if CHUNKS == 2:
+                state_pair(i)
+        if CHUNKS == 4:
+            state_pair(pairs // 4 + ch)
+    for load in loads[9:]:
+        load.wait()
+    project_near(c)
+    rest = list(range(3 * pairs // 4 if CHUNKS != 4 else pairs // 4 + 4, pairs))
+    for ch in range(CHUNKS):
+        forward(3, ch)
+        if ch == CHUNKS // 2 - 1:
+            for j in range(CHUNKS):
+                x_arrival(near, j).wait_recv()
+            project_near(oc)
+        if ch == 0:
+            for i in rest:
+                state_pair(i)
+    for ch in range(CHUNKS):
+        project_far(ch)
 
     r_col = cols_ref[:, r_at : r_at + 1]
     their_r = jnp.broadcast_to(info_in[0:1], (128, rows)).T[:, 0:1]
     for ch in range(CHUNKS):
         part_copy(ch).wait_recv()
         kvpart_copy(ch).wait_recv()
-    q_all[...] = ((own_q[...] + part_in[:, :q_cols].astype(F32)) * r_col).astype(BF16)
-    kv_all[c] = ((own_kv[c] + part_in[:, q_cols:].astype(F32)) * r_col).astype(BF16)
-    kv_all[oc] = ((own_kv[oc] + kvpart_in[...].astype(F32)) * their_r).astype(BF16)
+    ours = (sums_q[c] + part_in[...].astype(F32)) * r_col
+    q_all[...] = ours[:, :q_cols].astype(BF16)
+    kv_all[c] = ours[:, q_cols:].astype(BF16)
+    kv_all[oc] = ((sums_q[oc, :, q_cols:] + kvpart_in[...].astype(F32)) * their_r).astype(BF16)
 
     key_pos = lax.broadcasted_iota(jnp.int32, (rows, 2 * rows), 1)
     query_pos = c * rows + lax.broadcasted_iota(jnp.int32, (rows, 2 * rows), 0)
@@ -686,7 +719,7 @@
         ) * (HD ** (-0.5))
         scores = jnp.where(wanted, scores, -1e30)
         top = jnp.max(scores, axis=1, keepdims=True)
-        probs = jnp.where(wanted, jnp.exp(scores - top), 0.0)
+        probs = jnp.exp(scores - top)
         denom = jnp.sum(probs, axis=1, keepdims=True)
         mixed = (dot(probs.astype(BF16), values) / denom).astype(BF16)
         attended = (h_ref[:, lanes].astype(F32) + mixed.astype(F32)).astype(BF16)
@@ -764,12 +797,20 @@
     out, passed = pl.pallas_call(
         kernel,
         out_shape=(shape, shape),
-        in_specs=[vmem] * 4 + [anywhere] * 3 + [vmem] * 5,
+        in_specs=[anywhere] * 12,
         out_specs=(vmem, vmem),
         scratch_shapes=[
+            pltpu.VMEM((rows, width), BF16),
+            pltpu.VMEM((1, width), F32),
+            pltpu.VMEM((2 * n_state, width), BF16),
+            pltpu.VMEM((heads * tps, width), BF16),
+            pltpu.VMEM((1, rows), jnp.int32),
+            pltpu.VMEM((1, 1), jnp.int32),
+            pltpu.VMEM((1, heads), F32),
+            pltpu.VMEM((1, heads), F32),
+            pltpu.VMEM((1, heads), F32),
             pltpu.VMEM((2, tps, rows, width), BF16),
-            pltpu.VMEM((depth, q_cols), BF16),
-            pltpu.VMEM((2, depth, kv_cols), BF16),
+            pltpu.VMEM((depth, q_cols + 2 * kv_cols), BF16),
             pltpu.VMEM((rows, width), BF16),
             pltpu.VMEM((8, rows), F32),
             pltpu.VMEM((tps, 8, rows), F32),
@@ -783,8 +824,7 @@
             pltpu.VMEM((rows, q_cols + 2 * kv_cols), BF16),
             pltpu.VMEM((rows, 2 * kv_cols), BF16),
             pltpu.VMEM((rows, 2 * kv_cols), BF16),
-            pltpu.VMEM((rows, q_cols), F32),
-            pltpu.VMEM((2, rows, 2 * kv_cols), F32),
+            pltpu.VMEM((2, rows, q_cols + 2 * kv_cols), F32),
             pltpu.VMEM((2, rows, 2 * kv_cols), BF16),
             pltpu.VMEM((rows, q_cols), BF16),
             pltpu.VMEM((rows, width), BF16),
@@ -794,7 +834,7 @@
             pltpu.VMEM((2, rows, rows), F32),
             pltpu.VMEM((4, rows, width // 4), BF16),
             pltpu.VMEM((4, rows, width // 4), BF16),
-            dma((3,)),
+            dma((12,)),
             dma((tps, CHUNKS)),
             dma((tps, CHUNKS)),
             dma((tps // 2, CHUNKS)),
@@ -812,7 +852,7 @@
             dma((4,)),
         ],
         compiler_params=pltpu.CompilerParams(
-            collective_id=0, has_side_effects=True, vmem_limit_bytes=40 * 2**20
+            collective_id=0, has_side_effects=True, vmem_limit_bytes=60 * 2**20
         ),
         cost_estimate=pl.CostEstimate(
             flops=4 * rows * depth * (q_cols + 2 * kv_cols),
@@ -821,17 +861,17 @@
         ),
     )(
         hidden_in[0],
+        norm_gain,
+        bc_weight[0].T,
+        dt_weight[0].T,
         doc_ids[None],
         layer_kind[None],
-        norm_gain,
+        dt_bias,
+        decay_rate,
+        skip_gain,
         q_weight[0],
         k_weight[0],
         v_weight[0],
-        bc_weight[0],
-        dt_weight[0],
-        dt_bias,
-        decay_rate,
-        skip_gain,
     )
     return out[None], passed[None]
 

time: 61.3 us -> 46.4 us (0.76)
  local copies, waits for them, and re-layouts: 12 us -> 3.34 us
  Pallas kernels: 47.5 us -> 41.5 us
    unnamed x22 -> x2, local copies, waits for them, and re-layouts: 12 us -> 3.34 us
    pallas_call x1, Pallas kernels: 47.5 us -> 41.5 us  [fused(): pl.pallas_call(kernel, out_shape=(shape, shape), in_specs=[anywhere] * 12...]
where the time goes in v2:
time: 46.4 us; the launch traced here: 46.1 us
  Pallas kernels  41.5 us (89%)
  local copies, waits for them, and re-layouts  3.34 us (7%)
  between operations  1.29 us (3%)
    pallas_call x1, Pallas kernels, fused(): pl.pallas_call(kernel, out_shape=(shape, shape), in_specs=[anywhere] * 12...  41.5 us
    unnamed x2, local copies, waits for them, and re-layouts  3.34 us

profile of v2, /device:TPU:1, one launch (start us, length us, event | category | flops | bytes accessed | tf_op | source)
XLA Modules:
  0.0 46.1 jit_solution(11134623340374438253)
XLA Ops:
  1.3 41.5 %shard_map.131 = (bf16[128,1024]{1,0:T(8,128)(2,1)}, bf16[128,1024]{1,0:T(8,128)(2,1)}) custom-call(bf16[128,1024]{1,0:T(8,128)(2,1)} %bitcast.18, f32[1,1024]{1,0:T(1,128)} %gain_hbm.1, bf16[32,1024]{1,0:T(8,128)(2,1)} %bitcast.22, bf16[64,1024]{1,0:T(8,128)(2,1)} %bitcast.21, s32[1,128]{1,0:T(1,128)} %bitcast.23, s32[1,1]{1,0:T(1,128)} %bitcast.14.kind_hbm, ...), custom_call_target="tpu_custom_call" | custom-call | flops 1342177280 | bytes 5242880 | tf_op jit(solution)/shard_map/pallas_call | solution.py:797
  42.7 1.7 %copy.17 = bf16[1,128,1024]{2,1,0:T(8,128)(2,1)} copy(bf16[1,128,1024]{2,1,0:T(8,128)(2,1)} %bitcast.20) | data formatting | bytes 524288
  44.4 1.7 %copy.18 = bf16[1,128,1024]{2,1,0:T(8,128)(2,1)} copy(bf16[1,128,1024]{2,1,0:T(8,128)(2,1)} %bitcast.19) | data formatting | bytes 524288

commit v3 on v2

--- a/solution.py
+++ b/solution.py
@@ -269,8 +269,8 @@
     q_hbm,
     k_hbm,
     v_hbm,
-    out_ref,
-    passed_ref,
+    out_hbm,
+    passed_hbm,
     h_ref,
     gain_ref,
     bc_ref,
@@ -306,11 +306,10 @@
     prod,
     prev,
     w_sem,
-    right_sem,
-    left_sem,
+    ahead_sem,
+    behind_sem,
     across_sem,
-    z_recv,
-    x_recv,
+    b_recv,
     squares_ssem,
     squares_rsem,
     sums_ssem,
@@ -319,8 +318,10 @@
     small_rsem,
     part_ssem,
     part_rsem,
+    kvpart_sem,
     pipe_ssem,
     pipe_rsem,
+    out_sem,
 ):
     p, c, t = lax.axis_index("pipe"), lax.axis_index("ctx"), lax.axis_index("tp")
     pipes, tps = lax.axis_size("pipe"), lax.axis_size("tp")
@@ -389,60 +390,56 @@
     def span(ch):
         return pl.ds(ch * step_rows, step_rows)
 
-    def to_tp(b, ch, target, sem):
-        ref = blocks.at[c, b, span(ch)]
+    turn = 1 - 2 * c
+    place = c * (tps - 1) + t * turn
+
+    def block_at(kind, e):
+        return (c if kind == "O" else oc), c * (tps - 1) + e * turn
+
+    def block_copy(item, ch, sem, device):
+        tok, b = block_at(*item)
+        ref = blocks.at[tok, b, span(ch)]
         return pltpu.make_async_remote_copy(
-            ref, ref, sem, z_recv.at[b, ch], device_id={"tp": target}, device_id_type=MESH
-        )
-
-    def to_ctx(b, ch):
-        ref = blocks.at[c, b, span(ch)]
-        j = lax.rem(b, half)
-        return pltpu.make_async_remote_copy(
-            ref,
-            ref,
-            across_sem.at[j, ch],
-            x_recv.at[j, ch],
-            device_id={"ctx": oc},
-            device_id_type=MESH,
-        )
-
-    def send_right(d, ch, go=True):
-        @pl.when((t - d >= 0) & (t < tps - 1))
+            ref, ref, sem, b_recv.at[tok, b, ch], device_id=device, device_id_type=MESH
+        )
+
+    O0, O1, O2, O3, F0, F1 = ("O", 0), ("O", 1), ("O", 2), ("O", 3), ("F", 0), ("F", 1)
+    ahead, behind = (O0, O1, F0), (O1, O2, F1)
+
+    def ahead_copy(item, ch):
+        return block_copy(item, ch, ahead_sem.at[ahead.index(item), ch], {"tp": t + turn})
+
+    def behind_copy(item, ch):
+        return block_copy(item, ch, behind_sem.at[behind.index(item), ch], {"tp": t - turn})
+
+    def across_copy(item, ch):
+        return block_copy(item, ch, across_sem.at[ch], {"ctx": oc})
+
+    def own_sends(ch):
+        @pl.when(place == 0)
         def _():
-            copy = to_tp(t - d, ch, t + 1, right_sem.at[d, ch])
-            copy.start() if go else copy.wait_send()
-
-    def send_left(d, ch, go=True):
-        @pl.when((t + d < tps) & (t > 0))
+            ahead_copy(O0, ch).start()
+
+        @pl.when(place == 1)
         def _():
-            copy = to_tp(t + d, ch, t - 1, left_sem.at[d, ch])
-            copy.start() if go else copy.wait_send()
-
-    def send_across(b, ch):
-        @pl.when((b >= 0) & (b < tps) & (b // half == oc))
+            behind_copy(O1, ch).start()
+            ahead_copy(O1, ch).start()
+
+        @pl.when(place == 2)
         def _():
-            to_ctx(b, ch).start()
-
-    def own_sends(ch):
-        send_right(0, ch)
-        send_left(0, ch)
-        send_across(t, ch)
-
-    def forward(d, ch):
-        @pl.when(t - d >= 0)
+            across_copy(O2, ch).start()
+            behind_copy(O2, ch).start()
+
+        @pl.when(place == 3)
         def _():
-            to_tp(t - d, ch, t, right_sem.at[0, ch]).wait_recv()
-
-        send_right(d, ch)
-        send_across(t - d, ch)
-
-        @pl.when(t + d < tps)
+            across_copy(O3, ch).start()
+
+    def arrive(item, at, ch, then=()):
+        @pl.when(place == at)
         def _():
-            to_tp(t + d, ch, t, left_sem.at[0, ch]).wait_recv()
-
-        send_left(d, ch)
-        send_across(t + d, ch)
+            block_copy(item, ch, across_sem.at[ch], {"ctx": oc}).wait_recv()
+            for onward in then:
+                onward(item, ch).start()
 
     def gathered(out, into, ssem, rsem, k, mine):
         source = out.at[k] if len(out.shape) == 3 else out
@@ -592,99 +589,88 @@
         lanes = slice(i * 2 * channels, (i + 1) * 2 * channels)
         state_res[:, lanes] = (h_ref[:, lanes].astype(F32) + z).astype(BF16)
 
-    near = jnp.clip(t, half * c, half * c + half - 1) - half * c
-    far = half - 1 - near
-
-    def weight_rows(j, column):
-        return weight[pl.ds(pl.multiple_of(j * width, width), width), column : column + 256]
-
-    def project_near(tok):
-        x = blocks[tok, half * c + near]
-        for column in range(0, all_cols, 256):
-            sums_q[tok, :, column : column + 256] = dot(x, weight_rows(near, column))
+    first_half = half * c
+
+    def project(x, j, column):
+        depth = slice(j * width, (j + 1) * width)
+        return dot(x, weight[depth, column : column + 256])
+
+    def project_ours():
+        x = [blocks[c, first_half + j] for j in range(half)]
+        for column in (*range(q_cols, all_cols, 256), *range(0, q_cols, 256)):
+            value = sum([project(x[j], j, column) for j in range(1, half)], project(x[0], 0, column))
+            sums_q[c, :, column : column + 256] = value
+            if column == q_cols:
+                kvpart_out[...] = value.astype(BF16)
+                kvpart_copy().start()
 
     def part_copy(ch):
         return pltpu.make_async_remote_copy(
             part_out.at[span(ch)],
             part_in.at[span(ch)],
-            part_ssem.at[0, ch],
-            part_rsem.at[0, ch],
+            part_ssem.at[ch],
+            part_rsem.at[ch],
             device_id={"ctx": oc},
             device_id_type=MESH,
         )
 
-    def kvpart_copy(ch):
+    def kvpart_copy():
         return pltpu.make_async_remote_copy(
-            kvpart_out.at[span(ch)],
-            kvpart_in.at[span(ch)],
-            part_ssem.at[1, ch],
-            part_rsem.at[1, ch],
+            kvpart_out,
+            kvpart_in,
+            kvpart_sem.at[0],
+            kvpart_sem.at[1],
             device_id={"ctx": oc},
             device_id_type=MESH,
         )
 
-    def x_arrival(j, ch):
-        ref = blocks.at[oc, half * c + j, span(ch)]
-        return pltpu.make_async_remote_copy(
-            ref,
-            ref,
-            across_sem.at[j, ch],
-            x_recv.at[j, ch],
-            device_id={"ctx": oc},
-            device_id_type=MESH,
-        )
-
-    def project_far(ch):
-        x_arrival(far, ch).wait_recv()
-        block = half * c + far
-        x = jnp.concatenate([blocks[oc, block, span(ch)], blocks[c, block, span(ch)]], axis=0)
-        for column in (*range(q_cols, all_cols, 256), *range(0, q_cols, 256)):
-            lanes = slice(column, column + 256)
-            value = dot(x, weight_rows(far, column))
-            theirs = value[:step_rows] + sums_q[oc, span(ch), lanes]
-            ours = value[step_rows:] + sums_q[c, span(ch), lanes]
-            part_out[span(ch), lanes] = theirs.astype(BF16)
-            sums_q[c, span(ch), lanes] = ours
-            if column >= q_cols:
-                sums_q[oc, span(ch), lanes] = theirs
-                kvpart_out[span(ch)] = ours.astype(BF16)
-                kvpart_copy(ch).start()
+    def project_theirs(ch):
+        x = [blocks[oc, first_half + j, span(ch)] for j in range(half)]
+        for column in range(0, all_cols, 256):
+            value = sum([project(x[j], j, column) for j in range(1, half)], project(x[0], 0, column))
+            part_out[span(ch), column : column + 256] = value.astype(BF16)
+            if column == q_cols:
+                sums_q[oc, span(ch), column : column + 256] = value
         part_copy(ch).start()
 
     for ch in range(CHUNKS):
-        forward(1, ch)
+        arrive(F0, 0, ch, (ahead_copy,))
+        arrive(F1, 1, ch, (behind_copy,))
+        arrive(O2, 1, ch, (behind_copy, across_copy))
+        arrive(O0, 1, ch, (ahead_copy,))
+        arrive(O1, 2, ch, (ahead_copy,))
+        arrive(O1, 0, ch)
     info_copy.wait_recv()
     state_copy.wait_recv()
     for i in range(0, pairs // 4):
         state_pair(i)
     for ch in range(CHUNKS):
-        forward(2, ch)
-        for i in range(pairs // 4 + ch * pairs // 4, pairs // 4 + (ch + 1) * pairs // 4):
-            if CHUNKS == 2:
-                state_pair(i)
-        if CHUNKS == 4:
-            state_pair(pairs // 4 + ch)
+        arrive(O2, 0, ch, (across_copy,))
+        arrive(F0, 1, ch, (ahead_copy,))
+        arrive(O0, 2, ch, (ahead_copy,))
+        arrive(O1, 3, ch)
+        for i in range(pairs // 4 * (CHUNKS + ch) // CHUNKS, pairs // 4 * (CHUNKS + ch + 1) // CHUNKS):
+            state_pair(i)
     for load in loads[9:]:
         load.wait()
-    project_near(c)
-    rest = list(range(3 * pairs // 4 if CHUNKS != 4 else pairs // 4 + 4, pairs))
     for ch in range(CHUNKS):
-        forward(3, ch)
-        if ch == CHUNKS // 2 - 1:
-            for j in range(CHUNKS):
-                x_arrival(near, j).wait_recv()
-            project_near(oc)
-        if ch == 0:
-            for i in rest:
-                state_pair(i)
+        arrive(F0, 2, ch, (ahead_copy,))
+        arrive(O0, 3, ch)
+        for i in range(pairs // 2 * (CHUNKS + ch) // CHUNKS, pairs // 2 * (CHUNKS + ch + 1) // CHUNKS):
+            state_pair(i)
+    project_ours()
     for ch in range(CHUNKS):
-        project_far(ch)
+        arrive(F1, 0, ch)
+        arrive(F1, 2, ch)
+        arrive(F1, 3, ch)
+        arrive(F0, 3, ch)
+        project_theirs(ch)
 
     r_col = cols_ref[:, r_at : r_at + 1]
+    kvpart_copy().wait_recv()
     their_r = jnp.broadcast_to(info_in[0:1], (128, rows)).T[:, 0:1]
     for ch in range(CHUNKS):
         part_copy(ch).wait_recv()
-        kvpart_copy(ch).wait_recv()
     ours = (sums_q[c] + part_in[...].astype(F32)) * r_col
     q_all[...] = ours[:, :q_cols].astype(BF16)
     kv_all[c] = ours[:, q_cols:].astype(BF16)
@@ -711,6 +697,16 @@
             device_id={"pipe": p + 1},
             device_id_type=MESH,
         )
+
+    span_p = prod.shape[2]
+
+    def out_copy(k):
+        lanes = pl.ds(k * span_p, span_p)
+        return pltpu.make_async_copy(prod.at[k], out_hbm.at[:, lanes], out_sem.at[0, k])
+
+    def passed_copy(k):
+        lanes = pl.ds(k * span_p, span_p)
+        return pltpu.make_async_copy(prev.at[k], passed_hbm.at[:, lanes], out_sem.at[1, k])
 
     for head in range(q_heads):
         lanes = slice(head * HD, (head + 1) * HD)
@@ -728,45 +724,71 @@
             attended.astype(F32),
             state_res[:, lanes].astype(F32),
         ).astype(BF16)
-        out_ref[:, lanes] = result
         inner = head % per
         prod[head // per, :, inner * HD : (inner + 1) * HD] = result
         if inner == per - 1:
+            out_copy(head // per).start()
 
             @pl.when(p < pipes - 1)
             def _(k=head // per):
                 pipe_copy(k).start()
 
     for ch in range(CHUNKS):
-        for d in range(tps):
-            send_right(d, ch, False)
-            send_left(d, ch, False)
-        for j in range(half):
-            to_ctx(half * oc + j, ch).wait_send()
+        across_copy(O2, ch).wait_send()
+
+        @pl.when(place < 3)
+        def _(ch=ch):
+            ahead_copy(F0, ch).wait_send()
+            ahead_copy(O0, ch).wait_send()
+
+        @pl.when((place == 1) | (place == 2))
+        def _(ch=ch):
+            ahead_copy(O1, ch).wait_send()
+            behind_copy(O2, ch).wait_send()
+
+        @pl.when(place == 1)
+        def _(ch=ch):
+            behind_copy(O1, ch).wait_send()
+            behind_copy(F1, ch).wait_send()
+
         part_copy(ch).wait_send()
-        kvpart_copy(ch).wait_send()
+    kvpart_copy().wait_send()
     for k in peers:
         squares_copy(k, True).wait_send()
         sums_copy(k, True).wait_send()
     info_copy.wait_send()
     state_copy.wait_send()
 
-    span_p = prod.shape[2]
-
-    @pl.when(p > 0)
-    def _():
-        for k in range(q_heads // per):
-            pipe_copy(k).wait_recv()
-            passed_ref[:, k * span_p : (k + 1) * span_p] = prev[k]
-
     @pl.when(p == 0)
     def _():
-        passed_ref[...] = jnp.zeros(passed_ref.shape, BF16)
+        prev[...] = jnp.zeros(prev.shape, BF16)
+
+    for k in range(q_heads // per):
+
+        @pl.when(p > 0)
+        def _(k=k):
+            pipe_copy(k).wait_recv()
+
+        passed_copy(k).start()
+    for k in range(q_heads // per):
+        out_copy(k).wait()
+        passed_copy(k).wait()
 
     @pl.when(p < pipes - 1)
     def _():
         for k in range(q_heads // per):
             pipe_copy(k).wait_send()
+
+
+def deliver(out_from, passed_from, out_to, passed_to, sem):
+    copies = [
+        pltpu.make_async_copy(out_from, out_to, sem.at[0]),
+        pltpu.make_async_copy(passed_from, passed_to, sem.at[1]),
+    ]
+    for copy in copies:
+        copy.start()
+    for copy in copies:
+        copy.wait()
 
 
 def fused(
@@ -789,7 +811,6 @@
     heads = dt_bias.shape[1]
     n_state = bc_weight.shape[2] // 2
     tps = lax.axis_size("tp")
-    vmem = pl.BlockSpec(memory_space=pltpu.VMEM)
     anywhere = pl.BlockSpec(memory_space=pl.ANY)
     small = 2 * n_state + heads
     dma = pltpu.SemaphoreType.DMA
@@ -798,7 +819,7 @@
         kernel,
         out_shape=(shape, shape),
         in_specs=[anywhere] * 12,
-        out_specs=(vmem, vmem),
+        out_specs=(anywhere, anywhere),
         scratch_shapes=[
             pltpu.VMEM((rows, width), BF16),
             pltpu.VMEM((1, width), F32),
@@ -835,21 +856,22 @@
             pltpu.VMEM((4, rows, width // 4), BF16),
             pltpu.VMEM((4, rows, width // 4), BF16),
             dma((12,)),
-            dma((tps, CHUNKS)),
-            dma((tps, CHUNKS)),
-            dma((tps // 2, CHUNKS)),
-            dma((tps, CHUNKS)),
-            dma((tps // 2, CHUNKS)),
+            dma((3, CHUNKS)),
+            dma((3, CHUNKS)),
+            dma((CHUNKS,)),
+            dma((2, tps, CHUNKS)),
             dma((tps,)),
             dma((tps,)),
             dma((tps,)),
             dma((tps,)),
             dma((2,)),
             dma((2,)),
-            dma((2, CHUNKS)),
-            dma((2, CHUNKS)),
+            dma((CHUNKS,)),
+            dma((CHUNKS,)),
+            dma((2,)),
             dma((4,)),
             dma((4,)),
+            dma((2, 4)),
         ],
         compiler_params=pltpu.CompilerParams(
             collective_id=0, has_side_effects=True, vmem_limit_bytes=60 * 2**20
@@ -873,6 +895,13 @@
         k_weight[0],
         v_weight[0],
     )
+    out, passed = pl.pallas_call(
+        deliver,
+        out_shape=(shape, shape),
+        in_specs=[anywhere] * 2,
+        out_specs=(anywhere, anywhere),
+        scratch_shapes=[dma((2,))],
+    )(out, passed)
     return out[None], passed[None]
 
 

time: 46.4 us -> 59.9 us (1.29)
  Pallas kernels: 41.5 us -> 58.5 us
  local copies, waits for them, and re-layouts: 3.34 us -> 0 us
    pallas_call x0 -> x1, Pallas kernels: none -> 17 us  [fused(): pl.pallas_call(deliver, out_shape=(shape, shape), in_specs=[anywhere] * 2...]
    unnamed x2 -> x0, local copies, waits for them, and re-layouts: 3.34 us -> none
where the time goes in v3:
time: 59.9 us; the launch traced here: 59.8 us
  Pallas kernels  58.5 us (98%)
  between operations  1.29 us (2%)
    pallas_call x1, Pallas kernels, fused(): pl.pallas_call(kernel, out_shape=(shape, shape), in_specs=[anywhere] * 12...  41.5 us
    pallas_call x1, Pallas kernels, fused(): pl.pallas_call(deliver, out_shape=(shape, shape), in_specs=[anywhere] * 2...  17 us

profile of v3, /device:TPU:1, one launch (start us, length us, event | category | flops | bytes accessed | tf_op | source)
XLA Modules:
  0.0 59.8 jit_solution(6702607700491821802)
XLA Ops:
  1.3 41.5 %shard_map.131 = (bf16[128,1024]{1,0:T(8,128)(2,1)}, bf16[128,1024]{1,0:T(8,128)(2,1)}) custom-call(bf16[128,1024]{1,0:T(8,128)(2,1)} %bitcast.18, f32[1,1024]{1,0:T(1,128)} %gain_hbm.1, bf16[32,1024]{1,0:T(8,128)(2,1)} %bitcast.20, bf16[64,1024]{1,0:T(8,128)(2,1)} %bitcast.19, s32[1,128]{1,0:T(1,128)} %bitcast.21, s32[1,1]{1,0:T(1,128)} %bitcast.14.kind_hbm, ...), custom_call_target="tpu_custom_call" | custom-call | flops 1342177280 | bytes 5242880 | tf_op jit(solution)/shard_map/pallas_call | solution.py:818
  42.8 17.0 %shard_map.132 = (bf16[128,1024]{1,0:T(8,128)(2,1)}, bf16[128,1024]{1,0:T(8,128)(2,1)}) custom-call(bf16[128,1024]{1,0:T(8,128)(2,1)} %get-tuple-element.6.out_from, bf16[128,1024]{1,0:T(8,128)(2,1)} %get-tuple-element.7.passed_from), custom_call_target="tpu_custom_call" | custom-call | tf_op jit(solution)/shard_map/pallas_call | solution.py:898

commit v4 on v3

--- a/solution.py
+++ b/solution.py
@@ -235,7 +235,7 @@
     return (produced[None], moved[None])
 
 
-CHUNKS = 2
+CHUNKS = 4
 MESH = pl.DeviceIdType.MESH
 F32 = jnp.float32
 BF16 = jnp.bfloat16
@@ -462,7 +462,8 @@
     peers = [lax.rem(t + other, tps) for other in range(1, tps)]
     for k in peers:
         squares_copy(k, True).start()
-    own_sends(0)
+    for ch in range(CHUNKS // 2):
+        own_sends(ch)
     for k in peers:
         squares_copy(k, False).wait_recv()
     squares = squares_in[0]
@@ -498,8 +499,19 @@
         device_id_type=MESH,
     )
     info_copy.start()
-    for ch in range(1, CHUNKS):
+    for ch in range(CHUNKS // 2, CHUNKS):
         own_sends(ch)
+
+    def first_arrivals(ch):
+        arrive(F0, 0, ch, (ahead_copy,))
+        arrive(O2, 1, ch, (behind_copy, across_copy))
+        arrive(O0, 1, ch, (ahead_copy,))
+        arrive(F1, 1, ch, (behind_copy,))
+        arrive(O1, 2, ch, (ahead_copy,))
+        arrive(O1, 0, ch)
+
+    for ch in range(CHUNKS // 2):
+        first_arrivals(ch)
     for k in peers:
         sums_copy(k, False).wait_recv()
 
@@ -624,47 +636,61 @@
             device_id_type=MESH,
         )
 
-    def project_theirs(ch):
-        x = [blocks[oc, first_half + j, span(ch)] for j in range(half)]
+    early_block = block_at("F", jnp.where(place == 0, 0, 1))[1]
+    late_block = block_at("F", jnp.where(place == 0, 1, 0))[1]
+
+    def weight_rows(block, column):
+        start = pl.multiple_of((block - first_half) * width, width)
+        return weight[pl.ds(start, width), column : column + 256]
+
+    def project_early():
+        x = blocks[oc, early_block]
         for column in range(0, all_cols, 256):
-            value = sum([project(x[j], j, column) for j in range(1, half)], project(x[0], 0, column))
-            part_out[span(ch), column : column + 256] = value.astype(BF16)
+            sums_q[oc, :, column : column + 256] = dot(x, weight_rows(early_block, column))
+
+    def project_late(ch):
+        x = blocks[oc, late_block, span(ch)]
+        for column in range(0, all_cols, 256):
+            lanes = slice(column, column + 256)
+            value = sums_q[oc, span(ch), lanes] + dot(x, weight_rows(late_block, column))
+            part_out[span(ch), lanes] = value.astype(BF16)
             if column == q_cols:
-                sums_q[oc, span(ch), column : column + 256] = value
+                sums_q[oc, span(ch), lanes] = value
         part_copy(ch).start()
 
-    for ch in range(CHUNKS):
-        arrive(F0, 0, ch, (ahead_copy,))
-        arrive(F1, 1, ch, (behind_copy,))
-        arrive(O2, 1, ch, (behind_copy, across_copy))
-        arrive(O0, 1, ch, (ahead_copy,))
-        arrive(O1, 2, ch, (ahead_copy,))
-        arrive(O1, 0, ch)
+    for ch in range(CHUNKS // 2, CHUNKS):
+        first_arrivals(ch)
     info_copy.wait_recv()
     state_copy.wait_recv()
-    for i in range(0, pairs // 4):
-        state_pair(i)
+    done = 0
+
+    def state_until(upto):
+        for i in range(done, upto):
+            state_pair(i)
+        return upto
+
     for ch in range(CHUNKS):
         arrive(O2, 0, ch, (across_copy,))
         arrive(F0, 1, ch, (ahead_copy,))
         arrive(O0, 2, ch, (ahead_copy,))
         arrive(O1, 3, ch)
-        for i in range(pairs // 4 * (CHUNKS + ch) // CHUNKS, pairs // 4 * (CHUNKS + ch + 1) // CHUNKS):
-            state_pair(i)
+        done = state_until(pairs * (ch + 1) // (2 * CHUNKS))
     for load in loads[9:]:
         load.wait()
     for ch in range(CHUNKS):
         arrive(F0, 2, ch, (ahead_copy,))
+        done = state_until(pairs * (CHUNKS + ch + 1) // (2 * CHUNKS))
+    for ch in range(CHUNKS):
         arrive(O0, 3, ch)
-        for i in range(pairs // 2 * (CHUNKS + ch) // CHUNKS, pairs // 2 * (CHUNKS + ch + 1) // CHUNKS):
-            state_pair(i)
     project_ours()
     for ch in range(CHUNKS):
-        arrive(F1, 0, ch)
         arrive(F1, 2, ch)
         arrive(F1, 3, ch)
+    project_early()
+    for ch in range(CHUNKS):
+        arrive(F1, 0, ch)
         arrive(F0, 3, ch)
-        project_theirs(ch)
+        project_late(ch)
 
     r_col = cols_ref[:, r_at : r_at + 1]
     kvpart_copy().wait_recv()
@@ -780,14 +806,21 @@
             pipe_copy(k).wait_send()
 
 
-def deliver(out_from, passed_from, out_to, passed_to, sem):
-    copies = [
-        pltpu.make_async_copy(out_from, out_to, sem.at[0]),
-        pltpu.make_async_copy(passed_from, passed_to, sem.at[1]),
-    ]
-    for copy in copies:
+def deliver(out_from, passed_from, out_to, passed_to, held, sem):
+    rows = held.shape[1] // 2
+    arriving, leaving = [], []
+    for n, (source, into) in enumerate(((out_from, out_to), (passed_from, passed_to))):
+        for k in range(2):
+            part = pl.ds(k * rows, rows)
+            place = held.at[n, part]
+            arriving.append(pltpu.make_async_copy(source.at[part], place, sem.at[0, n, k]))
+            leaving.append(pltpu.make_async_copy(place, into.at[part], sem.at[1, n, k]))
+    for copy in arriving:
         copy.start()
-    for copy in copies:
+    for before, after in zip(arriving, leaving):
+        before.wait()
+        after.start()
+    for copy in leaving:
         copy.wait()
 
 
@@ -900,7 +933,8 @@
         out_shape=(shape, shape),
         in_specs=[anywhere] * 2,
         out_specs=(anywhere, anywhere),
-        scratch_shapes=[dma((2,))],
+        scratch_shapes=[pltpu.VMEM((2, rows, width), BF16), dma((2, 2, 2))],
+        compiler_params=pltpu.CompilerParams(vmem_limit_bytes=60 * 2**20),
     )(out, passed)
     return out[None], passed[None]
 

time: 59.9 us -> 43.8 us (0.73)
  Pallas kernels: 58.5 us -> 42.4 us
    pallas_call x1, Pallas kernels: 17 us -> 1.82 us  [fused(): pl.pallas_call(deliver, out_shape=(shape, shape), in_specs=[anywhere] * 2...]
    pallas_call x1, Pallas kernels: 41.5 us -> 40.6 us  [fused(): pl.pallas_call(kernel, out_shape=(shape, shape), in_specs=[anywhere] * 12...]
where the time goes in v4:
time: 43.8 us; the launch traced here: 43.7 us
  Pallas kernels  42.4 us (97%)
  between operations  1.29 us (3%)
    pallas_call x1, Pallas kernels, fused(): pl.pallas_call(kernel, out_shape=(shape, shape), in_specs=[anywhere] * 12...  40.6 us
    pallas_call x1, Pallas kernels, fused(): pl.pallas_call(deliver, out_shape=(shape, shape), in_specs=[anywhere] * 2...  1.82 us

profile of v4, /device:TPU:1, one launch (start us, length us, event | category | flops | bytes accessed | tf_op | source)
XLA Modules:
  0.0 43.7 jit_solution(337871501620215890)
XLA Ops:
  1.3 40.6 %shard_map.131 = (bf16[128,1024]{1,0:T(8,128)(2,1)}, bf16[128,1024]{1,0:T(8,128)(2,1)}) custom-call(bf16[128,1024]{1,0:T(8,128)(2,1)} %bitcast.18, f32[1,1024]{1,0:T(1,128)} %gain_hbm.1, bf16[32,1024]{1,0:T(8,128)(2,1)} %bitcast.20, bf16[64,1024]{1,0:T(8,128)(2,1)} %bitcast.19, s32[1,128]{1,0:T(1,128)} %bitcast.21, s32[1,1]{1,0:T(1,128)} %bitcast.14.kind_hbm, ...), custom_call_target="tpu_custom_call" | custom-call | flops 1342177280 | bytes 5242880 | tf_op jit(solution)/shard_map/pallas_call | solution.py:851
  41.9 1.8 %shard_map.132 = (bf16[128,1024]{1,0:T(8,128)(2,1)}, bf16[128,1024]{1,0:T(8,128)(2,1)}) custom-call(bf16[128,1024]{1,0:T(8,128)(2,1)} %get-tuple-element.6.out_from, bf16[128,1024]{1,0:T(8,128)(2,1)} %get-tuple-element.7.passed_from), custom_call_target="tpu_custom_call" | custom-call | tf_op jit(solution)/shard_map/pallas_call | solution.py:931

commit v5 on v4

--- a/solution.py
+++ b/solution.py
@@ -297,7 +297,6 @@
     kvpart_in,
     sums_q,
     kv_all,
-    q_all,
     state_res,
     cols_ref,
     rows_ref,
@@ -380,6 +379,7 @@
     gain = gain_ref[...]
     hg = (hf * gain).astype(BF16)
     blocks[c, t] = hg
+    kv_all[...] = jnp.zeros(kv_all.shape, BF16)
     squares = jnp.sum(hf * hf, axis=1, keepdims=True)
     squares_out[...] = jnp.broadcast_to(squares, (rows, 128)).T[0:8]
     squares_in[t] = squares_out[...]
@@ -692,72 +692,66 @@
         arrive(F0, 3, ch)
         project_late(ch)
 
-    r_col = cols_ref[:, r_at : r_at + 1]
     kvpart_copy().wait_recv()
     their_r = jnp.broadcast_to(info_in[0:1], (128, rows)).T[:, 0:1]
-    for ch in range(CHUNKS):
-        part_copy(ch).wait_recv()
-    ours = (sums_q[c] + part_in[...].astype(F32)) * r_col
-    q_all[...] = ours[:, :q_cols].astype(BF16)
-    kv_all[c] = ours[:, q_cols:].astype(BF16)
     kv_all[oc] = ((sums_q[oc, :, q_cols:] + kvpart_in[...].astype(F32)) * their_r).astype(BF16)
-
-    key_pos = lax.broadcasted_iota(jnp.int32, (rows, 2 * rows), 1)
-    query_pos = c * rows + lax.broadcasted_iota(jnp.int32, (rows, 2 * rows), 0)
     my_ids, their_ids = ids_row, info_in[8:9]
     at_first = jnp.where(c == 0, my_ids, their_ids)
     at_second = jnp.where(c == 0, their_ids, my_ids)
     key_ids = jnp.concatenate([at_first, at_second], axis=1)
-    wanted = (key_pos <= query_pos) & (key_ids == cols_ref[:, r_at + 8 : r_at + 9])
-    keys = kv_all[:, :, :HD].reshape(2 * rows, HD)
-    values = kv_all[:, :, HD:].reshape(2 * rows, HD)
-    attention = kind_ref[...] == 1
-    per = prod.shape[2] // HD
-
-    def pipe_copy(k):
+    key_pos = lax.broadcasted_iota(jnp.int32, (step_rows, 2 * rows), 1)
+    query_at = lax.broadcasted_iota(jnp.int32, (step_rows, 2 * rows), 0)
+    attention = jnp.broadcast_to(kind_ref[...] == 1, (step_rows, width))
+
+    def pipe_copy(ch):
         return pltpu.make_async_remote_copy(
-            prod.at[k],
-            prev.at[k],
-            pipe_ssem.at[k],
-            pipe_rsem.at[k],
+            prod.at[ch],
+            prev.at[ch],
+            pipe_ssem.at[ch],
+            pipe_rsem.at[ch],
             device_id={"pipe": p + 1},
             device_id_type=MESH,
         )
 
-    span_p = prod.shape[2]
-
-    def out_copy(k):
-        lanes = pl.ds(k * span_p, span_p)
-        return pltpu.make_async_copy(prod.at[k], out_hbm.at[:, lanes], out_sem.at[0, k])
-
-    def passed_copy(k):
-        lanes = pl.ds(k * span_p, span_p)
-        return pltpu.make_async_copy(prev.at[k], passed_hbm.at[:, lanes], out_sem.at[1, k])
-
-    for head in range(q_heads):
-        lanes = slice(head * HD, (head + 1) * HD)
+    def out_copy(ch):
+        return pltpu.make_async_copy(prod.at[ch], out_hbm.at[span(ch)], out_sem.at[0, ch])
+
+    def passed_copy(ch):
+        return pltpu.make_async_copy(prev.at[ch], passed_hbm.at[span(ch)], out_sem.at[1, ch])
+
+    for ch in range(CHUNKS):
+        part_copy(ch).wait_recv()
+        here = slice(ch * step_rows, (ch + 1) * step_rows)
+        ours = sums_q[c, span(ch)] + part_in[span(ch)].astype(F32)
+        ours = (ours * cols_ref[here, r_at : r_at + 1]).astype(BF16)
+        kv_all[c, span(ch)] = ours[:, q_cols:]
+        query = jnp.concatenate(
+            [ours[:, head * HD : (head + 1) * HD] for head in range(q_heads)], axis=0
+        )
+        keys = kv_all[:, :, :HD].reshape(2 * rows, HD)
+        values = kv_all[:, :, HD:].reshape(2 * rows, HD)
         scores = lax.dot_general(
-            q_all[:, lanes], keys, (((1,), (1,)), ((), ())), preferred_element_type=F32
+            query, keys, (((1,), (1,)), ((), ())), preferred_element_type=F32
         ) * (HD ** (-0.5))
-        scores = jnp.where(wanted, scores, -1e30)
+        wanted = (key_pos <= c * rows + ch * step_rows + query_at) & (
+            key_ids == cols_ref[here, r_at + 8 : r_at + 9]
+        )
+        barred = jnp.where(wanted, 0.0, -1e30)
+        scores = scores + jnp.concatenate([barred] * q_heads, axis=0)
         top = jnp.max(scores, axis=1, keepdims=True)
         probs = jnp.exp(scores - top)
         denom = jnp.sum(probs, axis=1, keepdims=True)
-        mixed = (dot(probs.astype(BF16), values) / denom).astype(BF16)
-        attended = (h_ref[:, lanes].astype(F32) + mixed.astype(F32)).astype(BF16)
-        result = jnp.where(
-            jnp.broadcast_to(attention, (rows, HD)),
-            attended.astype(F32),
-            state_res[:, lanes].astype(F32),
-        ).astype(BF16)
-        inner = head % per
-        prod[head // per, :, inner * HD : (inner + 1) * HD] = result
-        if inner == per - 1:
-            out_copy(head // per).start()
-
-            @pl.when(p < pipes - 1)
-            def _(k=head // per):
-                pipe_copy(k).start()
+        mixed = (dot(probs.astype(BF16), values) / denom).astype(BF16).astype(F32)
+        attended = jnp.concatenate(
+            [mixed[head * step_rows : (head + 1) * step_rows] for head in range(q_heads)], axis=1
+        )
+        attended = (h_ref[span(ch)].astype(F32) + attended).astype(BF16).astype(F32)
+        prod[ch] = jnp.where(attention, attended, state_res[span(ch)].astype(F32)).astype(BF16)
+        out_copy(ch).start()
+
+        @pl.when(p < pipes - 1)
+        def _(ch=ch):
+            pipe_copy(ch).start()
 
     for ch in range(CHUNKS):
         across_copy(O2, ch).wait_send()
@@ -789,20 +783,20 @@
     def _():
         prev[...] = jnp.zeros(prev.shape, BF16)
 
-    for k in range(q_heads // per):
+    for k in range(CHUNKS):
 
         @pl.when(p > 0)
         def _(k=k):
             pipe_copy(k).wait_recv()
 
         passed_copy(k).start()
-    for k in range(q_heads // per):
+    for k in range(CHUNKS):
         out_copy(k).wait()
         passed_copy(k).wait()
 
     @pl.when(p < pipes - 1)
     def _():
-        for k in range(q_heads // per):
+        for k in range(CHUNKS):
             pipe_copy(k).wait_send()
 
 
@@ -880,14 +874,13 @@
             pltpu.VMEM((rows, 2 * kv_cols), BF16),
             pltpu.VMEM((2, rows, q_cols + 2 * kv_cols), F32),
             pltpu.VMEM((2, rows, 2 * kv_cols), BF16),
-            pltpu.VMEM((rows, q_cols), BF16),
             pltpu.VMEM((rows, width), BF16),
             pltpu.VMEM((rows, 128), F32),
             pltpu.VMEM((2 * heads, rows), F32),
             pltpu.VMEM((rows, heads), F32),
             pltpu.VMEM((2, rows, rows), F32),
-            pltpu.VMEM((4, rows, width // 4), BF16),
-            pltpu.VMEM((4, rows, width // 4), BF16),
+            pltpu.VMEM((CHUNKS, rows // CHUNKS, width), BF16),
+            pltpu.VMEM((CHUNKS, rows // CHUNKS, width), BF16),
             dma((12,)),
             dma((3, CHUNKS)),
             dma((3, CHUNKS)),
@@ -902,9 +895,9 @@
             dma((CHUNKS,)),
             dma((CHUNKS,)),
             dma((2,)),
-            dma((4,)),
-            dma((4,)),
-            dma((2, 4)),
+            dma((CHUNKS,)),
+            dma((CHUNKS,)),
+            dma((2, CHUNKS)),
         ],
         compiler_params=pltpu.CompilerParams(
             collective_id=0, has_side_effects=True, vmem_limit_bytes=60 * 2**20

time: 43.8 us -> 42.4 us (0.968)
  Pallas kernels: 42.4 us -> 40.9 us
    pallas_call x1, Pallas kernels: 40.6 us -> 39.1 us  [fused(): pl.pallas_call(kernel, out_shape=(shape, shape), in_specs=[anywhere] * 12...]
where the time goes in v5:
time: 42.4 us; the launch traced here: 42.2 us
  Pallas kernels  40.9 us (96%)
  between operations  1.29 us (3%)
    pallas_call x1, Pallas kernels, fused(): pl.pallas_call(kernel, out_shape=(shape, shape), in_specs=[anywhere] * 12...  39.1 us
    pallas_call x1, Pallas kernels, fused(): pl.pallas_call(deliver, out_shape=(shape, shape), in_specs=[anywhere] * 2...  1.82 us

profile of v5, /device:TPU:1, one launch (start us, length us, event | category | flops | bytes accessed | tf_op | source)
XLA Modules:
  0.0 42.2 jit_solution(15552477913811033504)
XLA Ops:
  1.3 39.1 %shard_map.131 = (bf16[128,1024]{1,0:T(8,128)(2,1)}, bf16[128,1024]{1,0:T(8,128)(2,1)}) custom-call(bf16[128,1024]{1,0:T(8,128)(2,1)} %bitcast.18, f32[1,1024]{1,0:T(1,128)} %gain_hbm.1, bf16[32,1024]{1,0:T(8,128)(2,1)} %bitcast.20, bf16[64,1024]{1,0:T(8,128)(2,1)} %bitcast.19, s32[1,128]{1,0:T(1,128)} %bitcast.21, s32[1,1]{1,0:T(1,128)} %bitcast.14.kind_hbm, ...), custom_call_target="tpu_custom_call" | custom-call | flops 1342177280 | bytes 5242880 | tf_op jit(solution)/shard_map/pallas_call | solution.py:845
  40.4 1.8 %shard_map.132 = (bf16[128,1024]{1,0:T(8,128)(2,1)}, bf16[128,1024]{1,0:T(8,128)(2,1)}) custom-call(bf16[128,1024]{1,0:T(8,128)(2,1)} %get-tuple-element.6.out_from, bf16[128,1024]{1,0:T(8,128)(2,1)} %get-tuple-element.7.passed_from), custom_call_target="tpu_custom_call" | custom-call | tf_op jit(solution)/shard_map/pallas_call | solution.py:924

commit v6 on v5

--- a/solution.py
+++ b/solution.py
@@ -603,19 +603,6 @@
 
     first_half = half * c
 
-    def project(x, j, column):
-        depth = slice(j * width, (j + 1) * width)
-        return dot(x, weight[depth, column : column + 256])
-
-    def project_ours():
-        x = [blocks[c, first_half + j] for j in range(half)]
-        for column in (*range(q_cols, all_cols, 256), *range(0, q_cols, 256)):
-            value = sum([project(x[j], j, column) for j in range(1, half)], project(x[0], 0, column))
-            sums_q[c, :, column : column + 256] = value
-            if column == q_cols:
-                kvpart_out[...] = value.astype(BF16)
-                kvpart_copy().start()
-
     def part_copy(ch):
         return pltpu.make_async_remote_copy(
             part_out.at[span(ch)],
@@ -642,6 +629,24 @@
     def weight_rows(block, column):
         start = pl.multiple_of((block - first_half) * width, width)
         return weight[pl.ds(start, width), column : column + 256]
+
+    first_block = block_at("O", jnp.where(place == 0, 0, 1))[1]
+    second_block = block_at("O", jnp.where(place == 0, 1, 0))[1]
+
+    def project_first():
+        x = blocks[c, first_block]
+        for column in range(0, all_cols, 256):
+            sums_q[c, :, column : column + 256] = dot(x, weight_rows(first_block, column))
+
+    def project_second():
+        x = blocks[c, second_block]
+        for column in (*range(q_cols, all_cols, 256), *range(0, q_cols, 256)):
+            lanes = slice(column, column + 256)
+            value = sums_q[c, :, lanes] + dot(x, weight_rows(second_block, column))
+            sums_q[c, :, lanes] = value
+            if column == q_cols:
+                kvpart_out[...] = value.astype(BF16)
+                kvpart_copy().start()
 
     def project_early():
         x = blocks[oc, early_block]
@@ -677,12 +682,13 @@
         done = state_until(pairs * (ch + 1) // (2 * CHUNKS))
     for load in loads[9:]:
         load.wait()
+    project_first()
     for ch in range(CHUNKS):
         arrive(F0, 2, ch, (ahead_copy,))
         done = state_until(pairs * (CHUNKS + ch + 1) // (2 * CHUNKS))
     for ch in range(CHUNKS):
         arrive(O0, 3, ch)
-    project_ours()
+    project_second()
     for ch in range(CHUNKS):
         arrive(F1, 2, ch)
         arrive(F1, 3, ch)

time: 42.4 us -> 42.3 us (level)
  no operation moved by 1% of the time
where the time goes in v6:
time: 42.3 us; the launch traced here: 42.1 us
  Pallas kernels  40.8 us (96%)
  between operations  1.29 us (3%)
    pallas_call x1, Pallas kernels, fused(): pl.pallas_call(kernel, out_shape=(shape, shape), in_specs=[anywhere] * 12...  39 us
    pallas_call x1, Pallas kernels, fused(): pl.pallas_call(deliver, out_shape=(shape, shape), in_specs=[anywhere] * 2...  1.82 us

profile of v6, /device:TPU:1, one launch (start us, length us, event | category | flops | bytes accessed | tf_op | source)
XLA Modules:
  0.0 42.1 jit_solution(537931382395622484)
XLA Ops:
  1.3 39.0 %shard_map.131 = (bf16[128,1024]{1,0:T(8,128)(2,1)}, bf16[128,1024]{1,0:T(8,128)(2,1)}) custom-call(bf16[128,1024]{1,0:T(8,128)(2,1)} %bitcast.18, f32[1,1024]{1,0:T(1,128)} %gain_hbm.1, bf16[32,1024]{1,0:T(8,128)(2,1)} %bitcast.20, bf16[64,1024]{1,0:T(8,128)(2,1)} %bitcast.19, s32[1,128]{1,0:T(1,128)} %bitcast.21, s32[1,1]{1,0:T(1,128)} %bitcast.14.kind_hbm, ...), custom_call_target="tpu_custom_call" | custom-call | flops 1342177280 | bytes 5242880 | tf_op jit(solution)/shard_map/pallas_call | solution.py:851
  40.3 1.8 %shard_map.132 = (bf16[128,1024]{1,0:T(8,128)(2,1)}, bf16[128,1024]{1,0:T(8,128)(2,1)}) custom-call(bf16[128,1024]{1,0:T(8,128)(2,1)} %get-tuple-element.6.out_from, bf16[128,1024]{1,0:T(8,128)(2,1)} %get-tuple-element.7.passed_from), custom_call_target="tpu_custom_call" | custom-call | tf_op jit(solution)/shard_map/pallas_call | solution.py:930

commit v7 on v6

--- a/solution.py
+++ b/solution.py
@@ -514,6 +514,7 @@
         first_arrivals(ch)
     for k in peers:
         sums_copy(k, False).wait_recv()
+    first_arrivals(CHUNKS // 2)
 
     total = sums_in[0]
     for k in range(1, tps):
@@ -663,7 +664,7 @@
                 sums_q[oc, span(ch), lanes] = value
         part_copy(ch).start()
 
-    for ch in range(CHUNKS // 2, CHUNKS):
+    for ch in range(CHUNKS // 2 + 1, CHUNKS):
         first_arrivals(ch)
     info_copy.wait_recv()
     state_copy.wait_recv()

time: 42.3 us -> 42.5 us (level)
  no operation moved by 1% of the time
where the time goes in v7:
time: 42.5 us; the launch traced here: 42.3 us
  Pallas kernels  41.1 us (97%)
  between operations  1.29 us (3%)
    pallas_call x1, Pallas kernels, fused(): pl.pallas_call(kernel, out_shape=(shape, shape), in_specs=[anywhere] * 12...  39.2 us
    pallas_call x1, Pallas kernels, fused(): pl.pallas_call(deliver, out_shape=(shape, shape), in_specs=[anywhere] * 2...  1.82 us

profile of v7, /device:TPU:1, one launch (start us, length us, event | category | flops | bytes accessed | tf_op | source)
XLA Modules:
  0.0 42.3 jit_solution(13389807651362101587)
XLA Ops:
  1.3 39.2 %shard_map.131 = (bf16[128,1024]{1,0:T(8,128)(2,1)}, bf16[128,1024]{1,0:T(8,128)(2,1)}) custom-call(bf16[128,1024]{1,0:T(8,128)(2,1)} %bitcast.18, f32[1,1024]{1,0:T(1,128)} %gain_hbm.1, bf16[32,1024]{1,0:T(8,128)(2,1)} %bitcast.20, bf16[64,1024]{1,0:T(8,128)(2,1)} %bitcast.19, s32[1,128]{1,0:T(1,128)} %bitcast.21, s32[1,1]{1,0:T(1,128)} %bitcast.14.kind_hbm, ...), custom_call_target="tpu_custom_call" | custom-call | flops 1342177280 | bytes 5242880 | tf_op jit(solution)/shard_map/pallas_call | solution.py:852
  40.5 1.8 %shard_map.132 = (bf16[128,1024]{1,0:T(8,128)(2,1)}, bf16[128,1024]{1,0:T(8,128)(2,1)}) custom-call(bf16[128,1024]{1,0:T(8,128)(2,1)} %get-tuple-element.6.out_from, bf16[128,1024]{1,0:T(8,128)(2,1)} %get-tuple-element.7.passed_from), custom_call_target="tpu_custom_call" | custom-call | tf_op jit(solution)/shard_map/pallas_call | solution.py:931
